TPU v7x, 128 devices: a whole 4x4x4 slice. The times are simulated.
128 devices in a mesh: obs: 16 (over z, x), par: 8 (over y, core).
Axes of the slice: x: 4, y: 4, z: 4, core: 2. Of those that a mesh axis runs over, the one named last changes fastest.
Arguments:
- green: bfloat16 [65536, 16384], P('obs', 'par'), may hold values from -0.046875 to 0.046875
- blocks: int32 [512, 128], P('obs', 'par'), may hold values 0 or 1
- probes: bfloat16 [16384, 256], P('par'), may hold values from -6 to 6
- stations: int32 [65536], P(('obs', 'par')), may hold values from 0 to 127, as said below
- decay: float32 [128], P(('obs', 'par')), may hold values from 0.3 to 0.95
- noise_scale: float32 [128], P(('obs', 'par')), may hold values from 0.5 to 2
Outputs:
- sketch: float32 [256, 16384], P('obs', 'par')
Inputs may be any that keep to these rules, and one draw needn't show every extreme that they name: `stations`: within each device's aligned block of 512 rows no station appears more than 8 times, and one station appears exactly 8 times in every block.
All inputs are finite; a program needn't handle non-finite values. No bound on the sum of `blocks` on one device may be relied on, other than what follows from the above.
Results may differ from a plain program's by a relative error of at most 0.0025.
Values may be sent and summed in bfloat16 or wider, within the bound.
No kernel may reach another device: no remote copies, remote signals or barrier semaphores. Data moves between devices by JAX's collectives and lax.ppermute only.
A program may use at most 128 MiB of HBM per device.

v0:
```python
import jax
import jax.numpy as jnp
from jax import lax
from jax.sharding import PartitionSpec as P

BLK = 128


def local(green, blocks, probes, stations, decay, noise_scale):
    rows_dev, par_dev = green.shape
    columns = probes.shape[1]
    block_gate = blocks.astype(jnp.bfloat16)[:, None, :, None]
    masked = (green.reshape(rows_dev // BLK, BLK, par_dev // BLK, BLK) * block_gate).reshape(
        rows_dev, par_dev
    )
    obs_count = lax.axis_size("obs")
    par_count = lax.axis_size("par")
    dev_count = obs_count * par_count
    block_rows = rows_dev // par_count
    slot_count = max(2, 2 * block_rows // dev_count)
    forward = lax.psum_scatter(
        jnp.dot(masked, probes, preferred_element_type=jnp.float32),
        "par",
        scatter_dimension=0,
        tiled=True,
    ).astype(jnp.bfloat16)
    slot_total = dev_count * slot_count
    station_ids = jnp.arange(dev_count, dtype=jnp.int32)
    station_hits = (stations[:, None] == station_ids[None, :]).astype(jnp.int32)
    slot_index = jnp.sum((jnp.cumsum(station_hits, axis=0) - station_hits) * station_hits, axis=1)
    target_slot = stations * slot_count + slot_index
    positions = jnp.arange(slot_total, dtype=jnp.int32)
    placement = (positions[:, None] == target_slot[None, :]).astype(jnp.bfloat16)
    outgoing = (
        jnp.dot(placement, forward, preferred_element_type=jnp.float32)
        .astype(jnp.bfloat16)
        .reshape(dev_count, slot_count, columns)
    )
    filled = (
        jnp.sum(placement, axis=1, dtype=jnp.float32)
        .astype(jnp.bfloat16)
        .reshape(dev_count, slot_count)
    )
    arrived, present_flags = (
        lax.all_to_all(outgoing, ("obs", "par"), split_axis=0, concat_axis=0, tiled=True),
        lax.all_to_all(filled, ("obs", "par"), split_axis=0, concat_axis=0, tiled=True),
    )
    received_rows = arrived.reshape(slot_total, columns).astype(jnp.float32)
    filled_mask = present_flags.reshape(slot_total) > 0.5
    last_seen = lax.cummax(jnp.where(filled_mask, positions, -1), axis=0)
    prior_index = jnp.concatenate([jnp.full((1,), -1, jnp.int32), last_seen[:-1]])
    first_seen = lax.cummin(jnp.where(filled_mask, positions, slot_total), axis=0, reverse=True)
    next_index = jnp.concatenate([first_seen[1:], jnp.full((1,), slot_total, jnp.int32)])
    has_before = prior_index >= 0
    has_after = next_index < slot_total
    decay_rate = decay[0]
    noise_level = noise_scale[0]
    stationary = jnp.sqrt(1.0 - decay_rate * decay_rate)
    prior_rows = received_rows[jnp.clip(prior_index, 0, slot_total - 1)]
    whitened = (
        jnp.where(
            has_before[:, None], received_rows - decay_rate * prior_rows, stationary * received_rows
        )
        / noise_level
    )
    whitened = jnp.where(filled_mask[:, None], whitened, 0.0)
    following = jnp.where(
        has_after[:, None], whitened[jnp.clip(next_index, 0, slot_total - 1)], 0.0
    )
    leading = jnp.where(has_before, 1.0, stationary)[:, None]
    precision_rows = ((leading * whitened - decay_rate * following) / noise_level).astype(
        jnp.bfloat16
    )
    returned = lax.all_to_all(
        precision_rows.reshape(dev_count, slot_count, columns),
        ("obs", "par"),
        split_axis=0,
        concat_axis=0,
        tiled=True,
    )
    returned_flat = returned.reshape(slot_total, columns)
    own_rows = lax.dot_general(
        placement, returned_flat, (((0,), (0,)), ((), ())), preferred_element_type=jnp.float32
    ).astype(jnp.bfloat16)
    adjoint_part = lax.dot_general(
        lax.all_gather(own_rows, "par", axis=0, tiled=True),
        masked,
        (((0,), (0,)), ((), ())),
        preferred_element_type=jnp.float32,
    )
    return lax.psum_scatter(adjoint_part, "obs", scatter_dimension=0, tiled=True)


def solution(mesh):
    in_specs = (
        P("obs", "par"),
        P("obs", "par"),
        P("par", None),
        P(("obs", "par")),
        P(("obs", "par")),
        P(("obs", "par")),
    )
    out_specs = P("obs", "par")
    return jax.shard_map(local, mesh=mesh, in_specs=in_specs, out_specs=out_specs, check_vma=False)
```

profile of v0, /device:TPU:0, one launch (start us, length us, event | category | flops | bytes accessed | tf_op | source)
XLA Modules:
  0.0 244.8 jit_solution(9594638779588462346)
XLA Ops:
  6.5 0.0 copy-start
  6.5 0.0 reduce-scatter.3.cloned.1.call-start
  6.5 0.8 convert_element_type.40
  7.3 0.1 copy.29
  7.4 6.1 %mul.65 = bf16[32,128,16,128]{3,2,1,0:T(8,128)(2,1)} broadcast(bf16[32,16]{1,0:T(8,128)(2,1)S(1)} %copy.29), dimensions={0,2} | broadcast | bytes 16778240 | tf_op jit(solution)/shard_map/mul | solution.py:13
  13.6 0.0 copy-done
  13.6 0.0 copy-start.2
  13.6 16.0 %fusion.1 = f32[4096,256]{1,0:T(8,128)} fusion(bf16[2048,256]{1,0:T(8,128)(2,1)S(1)} %copy-done, bf16[4096,2048]{1,0:T(8,128)(2,1)} %param.6, bf16[512,8,16,128]{3,2,1,0:T(8,128)(2,1)} %bitcast.67), kind=kOutput, calls=%fused_computation.4 | convolution fusion | flops 4303355904 | bytes 38797312 | tf_op jit(solution)/shard_map/dot_general | solution.py:22
  29.6 0.0 reduce-scatter.3.cloned.1.call-update
  29.6 0.0 copy-done.2
  29.6 0.1 copy.23
  29.8 0.2 fusion.23
  30.1 0.2 fusion.21
  30.3 0.3 fusion.14
  30.6 0.8 all_to_all.16
  31.4 11.1 %all-to-all-start = ((bf16[128,1,8]{2,1,0:T(2,128)(2,1)}), bf16[128,1,8]{2,1,0:T(2,128)(2,1)S(1)}, u32[]{:S(2)}, u32[]{:S(2)}) async-start(bf16[128,1,8]{2,1,0:T(2,128)(2,1)} %all_to_all.16), calls=%async_computation | async-start | bytes 131072 | tf_op jit(solution)/shard_map/all_to_all | solution.py:46
  43.9 7.9 %all-to-all-done = bf16[128,1,8]{2,1,0:T(2,128)(2,1)S(1)} async-done(((bf16[128,1,8]{2,1,0:T(2,128)(2,1)}), bf16[128,1,8]{2,1,0:T(2,128)(2,1)S(1)}, u32[]{:S(2)}, u32[]{:S(2)}) %all-to-all-start) | async-done | bytes 2080 | tf_op jit(solution)/shard_map/all_to_all | solution.py:46
  51.8 0.1 copy.26
  51.8 0.1 copy.27
  52.0 0.1 gt.24
  52.1 0.1 gt.26
  52.2 0.3 reduce-window.26
  52.5 0.1 slice.28
  52.6 2.3 reduce-window.36
  54.9 0.1 slice_reduce_fusion
  55.1 0.1 minimum_bitcast_fusion
  55.1 0.1 slice.33
  55.2 0.1 slice_reduce_fusion.1
  55.3 0.1 maximum_bitcast_fusion
  55.4 0.1 compare_reduce_fusion.1
  55.5 0.1 ge.17
  55.6 0.1 compare_reduce_fusion
  55.7 0.1 lt.32
  55.8 0.1 copy.28
  55.9 0.1 compare_select_fusion.1
  56.0 0.1 compare_select_fusion
  56.1 14.5 %reduce-scatter.3.cloned.1.call-done = f32[512,256]{1,0:T(8,128)} async-done(((f32[4096,256]{1,0:T(8,128)}), f32[512,256]{1,0:T(8,128)}) %reduce-scatter.3.cloned.1.call-update) | async-done | bytes 524304 | tf_op jit(solution)/shard_map/reduce_scatter | solution.py:21
  70.6 2.3 fusion.6
  73.0 7.7 %all-to-all-start.1 = ((bf16[128,8,256]{2,1,0:T(8,128)(2,1)}), bf16[128,8,256]{2,1,0:T(8,128)(2,1)S(1)}, u32[]{:S(2)}, u32[]{:S(2)}) async-start(bf16[128,8,256]{2,1,0:T(8,128)(2,1)} %fusion.6), calls=%async_computation.2 | async-start | bytes 1048576 | tf_op jit(solution)/shard_map/all_to_all | solution.py:45
  80.7 0.0 all-gather.2.cloned.1.call-start
  80.8 0.1 add_compare_fusion
  80.9 13.4 %all-to-all-done.1 = bf16[128,8,256]{2,1,0:T(8,128)(2,1)S(1)} async-done(((bf16[128,8,256]{2,1,0:T(8,128)(2,1)}), bf16[128,8,256]{2,1,0:T(8,128)(2,1)S(1)}, u32[]{:S(2)}, u32[]{:S(2)}) %all-to-all-start.1) | async-done | bytes 524320 | tf_op jit(solution)/shard_map/all_to_all | solution.py:45
  94.2 0.0 copy-start.1
  94.2 0.8 copy-done.1
  95.1 0.1 convert_bitcast_fusion
  95.1 3.5 %gather_fusion = f32[1024,256]{1,0:T(8,128)S(1)} fusion(f32[1024,256]{1,0:T(8,128)S(1)} %convert_bitcast_fusion, s32[1024]{0:T(1024)S(1)} %broadcast_clamp_fusion.1), kind=kCustom, calls=%fused_computation | custom fusion | bytes 2101248 | tf_op jit(solution)/shard_map/gather | solution.py:59
  98.6 1.8 divide_select_fusion
  100.4 4.7 %gather_fusion.1 = f32[1024,256]{1,0:T(8,128)} fusion(f32[1024,256]{1,0:T(8,128)S(1)} %divide_select_fusion, s32[1024]{0:T(1024)S(1)} %broadcast_clamp_fusion), kind=kCustom, calls=%fused_computation.1 | custom fusion | bytes 2101248 | tf_op jit(solution)/shard_map/gather | solution.py:68
  105.1 2.7 %fusion.18 = bf16[128,8,256]{2,1,0:T(8,128)(2,1)S(1)} fusion(f32[1024,256]{1,0:T(8,128)} %gather_fusion.1, bf16[128,8,256]{2,1,0:T(8,128)(2,1)} %copy-done.1, f32[1024,256]{1,0:T(8,128)S(1)} %gather_fusion, f32[]{:T(128)} %bitcast.64, f32[]{:T(128)} %bitcast.65, f32[]{:T(128)S(6)} %sqrt.3, f32[128,8]{1,0:T(8,128)S(1)} %broadcast_select_fusion, ...), kind=kLoop, calls=%fused_computation.27 | loop fusion | flops 3407872 | bytes 3152908 | tf_op jit(solution)/shard_map/convert_element_type | solution.py:71
  107.7 17.9 %all_to_all.20 = bf16[128,8,256]{2,1,0:T(8,128)(2,1)S(1)} all-to-all(bf16[128,8,256]{2,1,0:T(8,128)(2,1)S(1)} %fusion.18), channel_id=1, replica_groups=mesh['obs'=16,'par'=8] {'obs','par'}, dimensions={0} | all-to-all | bytes 1048576 | tf_op jit(solution)/shard_map/all_to_all | solution.py:74
  125.6 1.5 fusion.7
  127.1 0.0 all-gather.2.cloned.1.call-update
  127.2 0.0 reduce-scatter.5.cloned.1.call-start
  127.2 21.2 %all-gather.2.cloned.1.call-done = bf16[4096,256]{1,0:T(8,128)(2,1)} async-done(((bf16[512,256]{1,0:T(8,128)(2,1)}), bf16[4096,256]{1,0:T(8,128)(2,1)}) %all-gather.2.cloned.1.call-update) | async-done | bytes 2097168 | tf_op jit(solution)/shard_map/all_gather | solution.py:86
  148.4 14.9 %fusion = f32[256,2048]{1,0:T(8,128)} fusion(bf16[4096,256]{1,0:T(8,128)(2,1)} %all-gather.2.cloned.1.call-done, bf16[4096,2048]{1,0:T(8,128)(2,1)} %param.6, bf16[512,8,16,128]{3,2,1,0:T(8,128)(2,1)} %bitcast.68), kind=kOutput, calls=%fused_computation.3 | convolution fusion | flops 4303355904 | bytes 37748736 | tf_op jit(solution)/shard_map/dot_general | solution.py:85
  163.3 0.0 reduce-scatter.5.cloned.1.call-update
  163.3 74.9 %reduce-scatter.5.cloned.1.call-done = f32[16,2048]{1,0:T(8,128)} async-done(((f32[256,2048]{1,0:T(8,128)}), f32[16,2048]{1,0:T(8,128)}) %reduce-scatter.5.cloned.1.call-update) | async-done | bytes 131088 | tf_op jit(solution)/shard_map/reduce_scatter | solution.py:91
  (15 shorter events, 0.2 us)
Async XLA Ops:
  6.5 7.0 %copy-start = (bf16[2048,256]{1,0:T(8,128)(2,1)S(1)}, bf16[2048,256]{1,0:T(8,128)(2,1)}, u32[]{:S(2)}) copy-start(bf16[2048,256]{1,0:T(8,128)(2,1)} %param.8) | copy-start | bytes 3145732
  6.5 64.1 %reduce-scatter.3.cloned.1.call-start = ((), (), s32[]{:S(2)}) async-start(), calls=%async_computation.5 | async-start | bytes 4718592 | tf_op jit(solution)/shard_map/reduce_scatter | solution.py:21
  13.6 16.1 %copy-start.2 = (s32[512]{0:T(512)S(1)}, s32[512]{0:T(512)}, u32[]{:S(2)}) copy-start(s32[512]{0:T(512)} %param.9) | copy-start | bytes 6148
  31.4 20.4 %all-to-all-start = ((bf16[128,1,8]{2,1,0:T(2,128)(2,1)}), bf16[128,1,8]{2,1,0:T(2,128)(2,1)S(1)}, u32[]{:S(2)}, u32[]{:S(2)}) async-start(bf16[128,1,8]{2,1,0:T(2,128)(2,1)} %all_to_all.16), calls=%async_computation | async-start | bytes 131072 | tf_op jit(solution)/shard_map/all_to_all | solution.py:46
  73.0 21.3 %all-to-all-start.1 = ((bf16[128,8,256]{2,1,0:T(8,128)(2,1)}), bf16[128,8,256]{2,1,0:T(8,128)(2,1)S(1)}, u32[]{:S(2)}, u32[]{:S(2)}) async-start(bf16[128,8,256]{2,1,0:T(8,128)(2,1)} %fusion.6), calls=%async_computation.2 | async-start | bytes 1048576 | tf_op jit(solution)/shard_map/all_to_all | solution.py:45
  80.7 67.7 %all-gather.2.cloned.1.call-start = ((), (), s32[]{:S(2)}) async-start(), calls=%async_computation.6 | async-start | bytes 2359296 | tf_op jit(solution)/shard_map/all_gather | solution.py:86
  94.2 0.8 copy-start.1
  127.2 111.1 %reduce-scatter.5.cloned.1.call-start = ((), (), s32[]{:S(2)}) async-start(), calls=%async_computation.7 | async-start | bytes 2228224 | tf_op jit(solution)/shard_map/reduce_scatter | solution.py:91
Sparse Core Ops, SparseCore 0:
  29.8 40.8 reduce-scatter.2
  127.3 21.0 all-gather.1
  163.4 74.7 reduce-scatter.4
where the time goes:
time: 245 us
  waiting for transfers between devices  132 us (54%)
  matrix products  34.7 us (14%)
  starting transfers between devices  19 us (8%)
  blocking collectives  17.9 us (7%)
  local copies, waits for them, and re-layouts  17.2 us (7%)
  between operations  14.6 us (6%)
  other arithmetic  9.38 us (4%)
    reduce_scatter x1, waiting for transfers between devices, local(): lax.psum_scatter(adjoint_part, 'obs', scatter_dimension=0, tiled=True)  74.9 us
    all_gather x1, waiting for transfers between devices, local(): lax.all_gather(own_rows, 'par', axis=0, tiled=True)  21.2 us
    all_to_all x1, blocking collectives, local(): lax.all_to_all(precision_rows.reshape(dev_count, slot_count, columns), ('...  17.9 us
    dot_general x1, matrix products, local(): jnp.dot(masked, probes, preferred_element_type=jnp.float32)  16 us
    dot_general x1, matrix products, local(): lax.dot_general(lax.all_gather(own_rows, 'par', axis=0, tiled=True), mask...  14.9 us
    reduce_scatter x1, waiting for transfers between devices, local(): lax.psum_scatter(jnp.dot(masked, probes, preferred_element_type=jnp.float...  14.5 us
    all_to_all x1, waiting for transfers between devices, local(): lax.all_to_all(outgoing, ('obs', 'par'), split_axis=0, concat_axis=0, til...  13.4 us
    all_to_all x1, starting transfers between devices, local(): lax.all_to_all(filled, ('obs', 'par'), split_axis=0, concat_axis=0, tiled...  11.1 us
  transfers between devices with their start and end apart: 5, of which 5 were waited for; matrix products, arithmetic and copies ran while one was open for 2% of the time, Pallas kernels for 0%

commit v1 on v0

v1 whole, which is shorter than its diff:
```python
import functools

import jax
import jax.numpy as jnp
from jax import lax
from jax.experimental import pallas as pl
from jax.experimental.pallas import tpu as pltpu
from jax.sharding import PartitionSpec as P

BLK = 128
CH = 256
AUG = 48
COLS = 32
BF = jnp.bfloat16
F32 = jnp.float32
NT = (((1,), (1,)), ((), ()))
MB = 1 << 20


def vm(mib):
    return pltpu.CompilerParams(vmem_limit_bytes=mib * MB)


def forward_kernel(idx, green, gate, probes, mine, send, acc):
    core = idx[0]
    parts = [green[r * BLK : (r + 1) * BLK, :] * gate[r].astype(BF) for r in range(4)]
    masked = jnp.concatenate(parts, axis=0)
    out = jnp.dot(masked, probes[...], preferred_element_type=F32)
    acc[...] = out.T
    mine[...] = acc[pl.ds(pl.multiple_of(core * 128, 128), 128), :]
    send[...] = acc[pl.ds(pl.multiple_of((1 - core) * 128, 128), 128), :]


def forward(idx, green, gate, probes):
    rows, par_dev = green.shape
    tile = 512
    return pl.pallas_call(
        forward_kernel,
        out_shape=[jax.ShapeDtypeStruct((128, rows), F32)] * 2,
        grid_spec=pltpu.PrefetchScalarGridSpec(
            num_scalar_prefetch=1,
            grid=(rows // tile,),
            in_specs=[
                pl.BlockSpec((tile, par_dev), lambda i, s: (i, 0)),
                pl.BlockSpec((tile // BLK, 1, par_dev), lambda i, s: (i, 0, 0)),
                pl.BlockSpec((par_dev, 256), lambda i, s: (0, 0)),
            ],
            out_specs=[pl.BlockSpec((128, tile), lambda i, s: (0, i))] * 2,
            scratch_shapes=[pltpu.VMEM((256, tile), F32)],
        ),
        compiler_params=vm(30),
        cost_estimate=pl.CostEstimate(
            flops=2 * rows * par_dev * 256, bytes_accessed=rows * par_dev * 2, transcendentals=0
        ),
        name="forward",
    )(idx, green, gate, probes)


def chain_kernel(st_row, st_col, phi, sigma, near, ends, coef):
    row = st_row[0]
    col = st_col[...]
    here = lax.broadcasted_iota(jnp.int32, (CH, CH), 0)
    there = lax.broadcasted_iota(jnp.int32, (CH, CH), 1)
    same = col == row
    prior = jnp.max(jnp.where(same & (here < there), here, -1), axis=0, keepdims=True)
    later = jnp.min(jnp.where(same & (here > there), here, CH), axis=0, keepdims=True)
    near[0] = jnp.where((here == prior) | (here == later), 1.0, 0.0).astype(BF)
    sid = lax.broadcasted_iota(jnp.int32, (128, CH), 0)
    hit = sid == row
    ends[0, :128, :] = jnp.where(hit & (prior < 0), 1.0, 0.0).astype(BF)
    ends[0, 128:, :] = jnp.where(hit & (later >= CH), 1.0, 0.0).astype(BF)
    rate = jnp.sum(jnp.where(hit, phi[...], 0.0), axis=0, keepdims=True)
    level = jnp.sum(jnp.where(hit, sigma[...], 0.0), axis=0, keepdims=True)
    scale = 1.0 / (level * level)
    coef[0:1, :] = (1.0 - rate * rate) * scale
    coef[1:2, :] = rate * rate * scale
    coef[2:3, :] = rate * scale
    coef[3:8, :] = jnp.zeros((5, CH), F32)


def chains(st_all, phi, sigma):
    rows = st_all.shape[0]
    n = rows // CH
    return pl.pallas_call(
        chain_kernel,
        out_shape=[
            jax.ShapeDtypeStruct((n, CH, CH), BF),
            jax.ShapeDtypeStruct((n, 256, CH), BF),
            jax.ShapeDtypeStruct((8, rows), F32),
        ],
        grid=(n,),
        in_specs=[
            pl.BlockSpec((1, 1, CH), lambda i: (i, 0, 0)),
            pl.BlockSpec((CH, 1), lambda i: (i, 0)),
            pl.BlockSpec((128, 1), lambda i: (0, 0)),
            pl.BlockSpec((128, 1), lambda i: (0, 0)),
        ],
        out_specs=[
            pl.BlockSpec((1, CH, CH), lambda i: (i, 0, 0)),
            pl.BlockSpec((1, 256, CH), lambda i: (i, 0, 0)),
            pl.BlockSpec((8, CH), lambda i: (0, i)),
        ],
        compiler_params=vm(16),
        name="chains",
    )(st_all.reshape(n, 1, CH), st_all.reshape(rows, 1), phi.reshape(128, 1), sigma.reshape(128, 1))


def ends_kernel(own, r1, r2, r3, ends, yaug, tips, pay):
    n = ends.shape[0]
    total = own[...] + r1[...].astype(F32) + r2[...].astype(F32) + r3[...].astype(F32)
    yaug[:COLS, :] = total.astype(BF)
    yaug[COLS:, :] = jnp.ones((AUG - COLS, total.shape[1]), BF)
    for b in range(n):
        tips[b] = lax.dot_general(
            yaug[:, b * CH : (b + 1) * CH], ends[b], NT, preferred_element_type=F32
        )
    first = jnp.zeros((AUG, 128), F32)
    last = jnp.zeros((AUG, 128), F32)
    for b in range(n):
        here = tips[b, :, 128:]
        last = jnp.where(here[COLS : COLS + 1, :] > 0.5, here, last)
        here = tips[n - 1 - b, :, :128]
        first = jnp.where(here[COLS : COLS + 1, :] > 0.5, here, first)
    pay[:AUG, :] = first.astype(BF)
    pay[AUG:, :] = last.astype(BF)


def chain_ends(own, recv, ends):
    rows = own.shape[1]
    n = rows // CH
    return pl.pallas_call(
        ends_kernel,
        out_shape=[
            jax.ShapeDtypeStruct((AUG, rows), BF),
            jax.ShapeDtypeStruct((n, AUG, 256), F32),
            jax.ShapeDtypeStruct((2 * AUG, 128), BF),
        ],
        in_specs=[pl.BlockSpec(memory_space=pltpu.VMEM)] * 5,
        out_specs=[pl.BlockSpec(memory_space=pltpu.VMEM)] * 3,
        compiler_params=vm(24),
        name="chain_ends",
    )(own, *recv, ends)


def nearest(me, buf, low, high):
    for j in range(4):
        last = buf[j, AUG:, :].astype(F32)
        ok = jnp.where(me > j, last[COLS : COLS + 1, :], 0.0) > 0.5
        low = jnp.where(ok, last, low)
        first = buf[3 - j, :AUG, :].astype(F32)
        ok = jnp.where(me < 3 - j, first[COLS : COLS + 1, :], 0.0) > 0.5
        high = jnp.where(ok, first, high)
    return low, high


def fill(me, buf, pay, recv):
    buf[me] = pay[...]
    for k, r in enumerate(recv):
        buf[lax.rem(me + 3 - k, 4)] = r[...]


def cross_kernel(idx, pay, r1, r2, r3, low, high, out, buf):
    me = idx[2]
    fill(me, buf, pay, (r1, r2, r3))
    zero = jnp.zeros((AUG, 128), F32)
    a, b = nearest(me, buf, zero, zero)
    low[...] = a
    high[...] = b
    last, _ = nearest(jnp.int32(4), buf, zero, zero)
    _, first = nearest(jnp.int32(-1), buf, zero, zero)
    out[:AUG, :] = first.astype(BF)
    out[AUG:, :] = last.astype(BF)


def cross(idx, pay, recv):
    return pl.pallas_call(
        cross_kernel,
        out_shape=[
            jax.ShapeDtypeStruct((AUG, 128), F32),
            jax.ShapeDtypeStruct((AUG, 128), F32),
            jax.ShapeDtypeStruct((2 * AUG, 128), BF),
        ],
        in_specs=[pl.BlockSpec(memory_space=pltpu.SMEM)] + [pl.BlockSpec(memory_space=pltpu.VMEM)] * 4,
        out_specs=[pl.BlockSpec(memory_space=pltpu.VMEM)] * 3,
        scratch_shapes=[pltpu.VMEM((4, 2 * AUG, 128), BF)],
        compiler_params=vm(8),
        name="cross",
    )(idx, pay, *recv)


def precision_kernel(idx, yaug, tips, near, ends, coef, low, high, pay, r1, r2, r3, out, buf, carry):
    n = near.shape[0]
    me = idx[3]
    fill(me, buf, pay, (r1, r2, r3))
    zero = jnp.zeros((AUG, 128), F32)
    below, above = nearest(me, buf, zero, zero)
    x_below, x_above = low[...], high[...]
    below = jnp.where(x_below[COLS : COLS + 1, :] > 0.5, x_below, below)
    above = jnp.where(x_above[COLS : COLS + 1, :] > 0.5, x_above, above)
    for b in range(n):
        carry[b, :, :128] = below.astype(BF)
        here = tips[b, :, 128:]
        below = jnp.where(here[COLS : COLS + 1, :] > 0.5, here, below)
        e = n - 1 - b
        carry[e, :, 128:] = above.astype(BF)
        here = tips[e, :, :128]
        above = jnp.where(here[COLS : COLS + 1, :] > 0.5, here, above)
    for b in range(n):
        at = slice(b * CH, (b + 1) * CH)
        y = yaug[:, at]
        around = jnp.dot(y, near[b], preferred_element_type=F32) + jnp.dot(
            carry[b], ends[b], preferred_element_type=F32
        )
        alpha = coef[0:1, at] + coef[1:2, at] * around[COLS : COLS + 1, :]
        out[:, at] = (alpha * y[:COLS, :].astype(F32) - coef[2:3, at] * around[:COLS, :]).astype(BF)


def precision(idx, yaug, tips, near, ends, coef, low, high, pay, recv):
    rows = yaug.shape[1]
    n = rows // CH
    return pl.pallas_call(
        precision_kernel,
        out_shape=jax.ShapeDtypeStruct((COLS, rows), BF),
        in_specs=[pl.BlockSpec(memory_space=pltpu.SMEM)] + [pl.BlockSpec(memory_space=pltpu.VMEM)] * 11,
        out_specs=pl.BlockSpec(memory_space=pltpu.VMEM),
        scratch_shapes=[pltpu.VMEM((4, 2 * AUG, 128), BF), pltpu.VMEM((n, AUG, 256), BF)],
        compiler_params=vm(24),
        name="precision",
    )(idx, yaug, tips, near, ends, coef, low, high, pay, *recv)


def adjoint_kernel(axis, idx, *refs):
    pieces, (green, gate) = refs[:8], refs[8:10]
    keep, s1, s2, s3 = refs[10:14]
    panel, acc = refs[14:]
    core, y = idx[0], idx[1]

    @pl.when(pl.program_id(0) == 0)
    def _():
        for k in range(4):
            spot = lax.rem(y + 4 - k, 4) * COLS
            panel[pl.ds(pl.multiple_of(core * 128 + spot, COLS), COLS), :] = pieces[k][...]
            panel[pl.ds(pl.multiple_of((1 - core) * 128 + spot, COLS), COLS), :] = pieces[4 + k][...]

    rows = green.shape[0]
    total = None
    for j in range(rows // 512):
        parts = [
            green[(4 * j + r) * BLK : (4 * j + r + 1) * BLK, :] * gate[4 * j + r].astype(BF)
            for r in range(4)
        ]
        part = jnp.dot(
            panel[:, j * 512 : (j + 1) * 512],
            jnp.concatenate(parts, axis=0),
            preferred_element_type=F32,
        )
        total = part if total is None else total + part
    acc[...] = total
    me = idx[2] if axis == "x" else idx[3]
    for k, ref in enumerate((keep, s1, s2, s3)):
        to = lax.rem(me + k, 4)
        for j in range(4):
            at = j * 64 + to * 16 if axis == "x" else to * 64 + j * 16
            ref[j] = acc[pl.ds(pl.multiple_of(at, 16), 16), :].astype(ref.dtype)


def adjoint(axis, half, idx, pieces, green, gate):
    rows, par_dev = green.shape
    tile = 512
    wide = par_dev // 2
    steps = wide // tile
    shape = (4, 16, wide)
    whole = pl.BlockSpec((COLS, rows), lambda i, s: (0, 0))
    return pl.pallas_call(
        functools.partial(adjoint_kernel, axis),
        out_shape=[jax.ShapeDtypeStruct(shape, F32)] + [jax.ShapeDtypeStruct(shape, BF)] * 3,
        grid_spec=pltpu.PrefetchScalarGridSpec(
            num_scalar_prefetch=1,
            grid=(steps,),
            in_specs=[whole] * 8
            + [
                pl.BlockSpec((rows, tile), lambda i, s: (0, half * steps + i)),
                pl.BlockSpec((rows // BLK, 1, tile), lambda i, s: (0, 0, half * steps + i)),
            ],
            out_specs=[pl.BlockSpec((4, 16, tile), lambda i, s: (0, 0, i))] * 4,
            scratch_shapes=[pltpu.VMEM((256, rows), BF), pltpu.VMEM((256, tile), F32)],
        ),
        compiler_params=vm(40),
        cost_estimate=pl.CostEstimate(
            flops=rows * par_dev * 256, bytes_accessed=rows * par_dev, transcendentals=0
        ),
        name="adjoint_" + axis,
    )(idx, *pieces, green, gate)


def y_shift(v, k):
    return lax.ppermute(v, "par", [(2 * y + c, 2 * ((y + k) % 4) + c) for y in range(4) for c in range(2)])


def core_swap(v):
    return lax.ppermute(v, "par", [(i, i ^ 1) for i in range(8)])


def x_shift(v, k):
    return lax.ppermute(v, "obs", [(4 * z + x, 4 * z + (x + k) % 4) for z in range(4) for x in range(4)])


def z_shift(v, k):
    return lax.ppermute(v, "obs", [(4 * z + x, 4 * ((z + k) % 4) + x) for z in range(4) for x in range(4)])


ORDER = (2, 1, 3)


def spread(shift, parts):
    got = {k: shift(parts[k], k) for k in ORDER}
    return [got[k] for k in (1, 2, 3)]


def pick(v, i):
    return lax.dynamic_index_in_dim(v, i, 0, keepdims=False)


def local(green, blocks, probes, stations, decay, noise_scale):
    par = lax.axis_index("par")
    obs = lax.axis_index("obs")
    core, y = par % 2, par // 2
    x, z = obs % 4, obs // 4
    idx = jnp.stack([core, y, x, z]).astype(jnp.int32)

    st_all = lax.all_gather(stations, "par", axis=0, tiled=True)
    slot = obs * 8 + par
    both = jnp.where(
        jnp.arange(128)[None, :] == slot, jnp.stack([decay, noise_scale]), 0.0
    )
    both = lax.psum(both, ("obs", "par"))
    near, ends, coef = chains(st_all, both[0], both[1])

    gate = jnp.repeat(blocks.astype(F32), BLK, axis=1)[:, None, :]
    mine, send = forward(idx, green, gate, probes)
    total = (mine + core_swap(send)).reshape(4, COLS, -1)
    parts = [pick(total, (y + k) % 4) for k in range(4)]
    recv = spread(y_shift, [None] + [p.astype(BF) for p in parts[1:]])
    yaug, tips, pay = chain_ends(parts[0], recv, ends)

    low, high, pay_z = cross(idx, pay, spread(x_shift, [pay] * 4))
    rows_t = precision(idx, yaug, tips, near, ends, coef, low, high, pay_z, spread(z_shift, [pay_z] * 4))

    pieces = [rows_t] + spread(y_shift, [rows_t] * 4)
    pieces = pieces + [core_swap(p) for p in pieces]

    outs = []
    for half, axis, one, two, where in (
        (0, "x", x_shift, z_shift, z),
        (1, "z", z_shift, x_shift, x),
    ):
        keep, *sends = adjoint(axis, half, idx, pieces, green, gate)
        got = spread(one, [None] + sends)
        mid = keep + got[0].astype(F32) + got[1].astype(F32) + got[2].astype(F32)
        parts = [pick(mid, (where + k) % 4) for k in range(4)]
        got = spread(two, parts)
        outs.append(parts[0] + got[0] + got[1] + got[2])
    return jnp.concatenate(outs, axis=1)


def solution(mesh):
    in_specs = (
        P("obs", "par"),
        P("obs", "par"),
        P("par", None),
        P(("obs", "par")),
        P(("obs", "par")),
        P(("obs", "par")),
    )
    out_specs = P("obs", "par")
    return jax.shard_map(local, mesh=mesh, in_specs=in_specs, out_specs=out_specs, check_vma=False)
```

time: 245 us -> 189 us (0.77)
  waiting for transfers between devices: 132 us -> 31.4 us
  blocking collectives: 17.9 us -> 80 us
  matrix products: 34.7 us -> 0 us
  Pallas kernels: 0 us -> 26.6 us
  starting transfers between devices: 19 us -> 36.1 us
  between operations: 14.6 us -> 1.52 us
  local copies, waits for them, and re-layouts: 17.2 us -> 9.58 us
  other arithmetic: 9.38 us -> 3.56 us
    reduce_scatter x2 -> x0, waiting for transfers between devices: 89.5 us -> none  [the longest x1 74.9 us: local(): lax.psum_scatter(adjoint_part, 'obs', scatter_dimension=0, tiled=True)]
    psum x0 -> x1, blocking collectives: none -> 68.7 us  [local(): both = lax.psum(both, ('obs', 'par'))]
    ppermute x0 -> x29, starting transfers between devices: none -> 36.1 us  [the longest x9 13.2 us: x_shift(): lax.ppermute(v, 'obs', [(4 * z + x, 4 * z + (x + k) % 4) for z in range(4...]
    dot_general x4 -> x0, matrix products: 34.7 us -> none  [the longest x1 16 us: local(): jnp.dot(masked, probes, preferred_element_type=jnp.float32)]
    ppermute x0 -> x29, waiting for transfers between devices: none -> 31.4 us  [the longest x6 19.1 us: y_shift(): lax.ppermute(v, 'par', [(2 * y + c, 2 * ((y + k) % 4) + c) for y in range...]
    pallas_call x0 -> x7, Pallas kernels: none -> 26.6 us  [the longest x2 11.2 us: adjoint(): pl.pallas_call(functools.partial(adjoint_kernel, axis), out_shape=[jax.Sh...]
    all_to_all x2 -> x0, waiting for transfers between devices: 21.3 us -> none  [the longest x1 13.4 us: local(): lax.all_to_all(outgoing, ('obs', 'par'), split_axis=0, concat_axis=0, til...]
    all_gather x1 -> x0, waiting for transfers between devices: 21.2 us -> none  [local(): lax.all_gather(own_rows, 'par', axis=0, tiled=True)]
  transfers between devices with their start and end apart: 5 -> 29, of which waited for: 5 -> 17; matrix products, arithmetic and copies ran while one was open for 2% -> 1% of each run, Pallas kernels for 0% -> 5%
where the time goes in v1:
time: 189 us
  blocking collectives  80 us (42%)
  starting transfers between devices  36.1 us (19%)
  waiting for transfers between devices  31.4 us (17%)
  Pallas kernels  26.6 us (14%)
  local copies, waits for them, and re-layouts  9.58 us (5%)
  other arithmetic  3.56 us (2%)
    psum x1, blocking collectives, local(): both = lax.psum(both, ('obs', 'par'))  68.7 us
    ppermute x6, waiting for transfers between devices, y_shift(): lax.ppermute(v, 'par', [(2 * y + c, 2 * ((y + k) % 4) + c) for y in range...  19.1 us
    ppermute x9, starting transfers between devices, x_shift(): lax.ppermute(v, 'obs', [(4 * z + x, 4 * z + (x + k) % 4) for z in range(4...  13.2 us
    ppermute x9, starting transfers between devices, z_shift(): lax.ppermute(v, 'obs', [(4 * z + x, 4 * ((z + k) % 4) + x) for z in range...  12.2 us
    all_gather x1, blocking collectives, local(): st_all = lax.all_gather(stations, 'par', axis=0, tiled=True)  11.2 us
    pallas_call x2, Pallas kernels, adjoint(): pl.pallas_call(functools.partial(adjoint_kernel, axis), out_shape=[jax.Sh...  11.2 us
    ppermute x6, starting transfers between devices, y_shift(): lax.ppermute(v, 'par', [(2 * y + c, 2 * ((y + k) % 4) + c) for y in range...  10.2 us
    unnamed x10, local copies, waits for them, and re-layouts  8.33 us
  transfers between devices with their start and end apart: 29, of which 17 were waited for; matrix products, arithmetic and copies ran while one was open for 1% of the time, Pallas kernels for 5%

profile of v1, /device:TPU:0, one launch (start us, length us, event | category | flops | bytes accessed | tf_op | source)
XLA Modules:
  0.0 188.7 jit_solution(11665646581995432526)
XLA Ops:
  0.0 0.7 convert_element_type.39
  0.7 0.1 copy.14
  0.8 0.1 pad_add_fusion.idx
  0.9 0.1 broadcast_in_dim.26
  1.0 5.8 %copy-done = bf16[4096,2048]{1,0:T(8,128)(2,1)S(1)} copy-done((bf16[4096,2048]{1,0:T(8,128)(2,1)S(1)}, bf16[4096,2048]{1,0:T(8,128)(2,1)}, u32[]{:S(2)}) %copy-start) | copy-done | bytes 16777240
  6.8 1.2 copy-done.3
  8.0 8.0 %forward.1 = (f32[128,4096]{1,0:T(8,128)S(1)}, f32[128,4096]{1,0:T(8,128)}) custom-call(s32[4]{0:T(128)S(1)} %pad_add_fusion.idx, bf16[4096,2048]{1,0:T(8,128)(2,1)S(1)} %copy-done, f32[32,1,2048]{2,1,0:T(1,128)S(1)} %bitcast.51, bf16[2048,256]{1,0:T(8,128)(2,1)S(1)} %copy-done.3), custom_call_target="tpu_custom_call" | custom-call | flops 4294967296 | bytes 16777216 | tf_op jit(solution)/shard_map/forward/pallas_call | solution.py:37
  16.0 1.3 copy-done.1
  18.7 0.1 maximum_bitcast_fusion
  18.8 68.7 %psum.7 = f32[2,128]{1,0:T(2,128)S(1)} all-reduce(f32[2,128]{1,0:T(2,128)S(1)} %broadcast_select_fusion), channel_id=1, replica_groups=mesh['obs'=16,'par'=8] {'obs','par'}, use_global_device_ids=true, to_apply=%region_0.1 | all-reduce | flops 256 | bytes 2048 | tf_op jit(solution)/shard_map/psum | solution.py:336
  87.6 0.1 copy.16.phi
  87.7 0.1 copy.17.sigma
  87.8 11.2 %all-gather = s32[8,1,512]{2,1,0:T(1,128)S(1)} all-gather(s32[1,1,512]{2,1,0:T(1,128)S(1)} %bitcast.58), channel_id=1, replica_groups=mesh['obs'=16,'par'=8] {'par'}, dimensions={0}, use_global_device_ids=true | all-gather | bytes 18432 | tf_op jit(solution)/shard_map/all_gather | solution.py:331
  99.0 0.6 copy.15.st_col
  99.7 4.5 %chains.1 = (bf16[16,256,256]{2,1,0:T(8,128)(2,1)S(1)}, bf16[16,256,256]{2,1,0:T(8,128)(2,1)S(1)}, f32[8,4096]{1,0:T(8,128)S(1)}) custom-call(s32[16,1,256]{2,1,0:T(1,128)S(1)} %bitcast.55, s32[4096,1]{1,0:T(8,128)S(1)} %copy.15.st_col, f32[128,1]{1,0:T(8,128)S(1)} %copy.16.phi, f32[128,1]{1,0:T(8,128)S(1)} %copy.17.sigma), custom_call_target="tpu_custom_call" | custom-call | tf_op jit(solution)/shard_map/chains/pallas_call | solution.py:84
  104.2 1.8 add.156
  106.0 0.1 fusion.2
  106.2 2.5 %collective-permute-start.2 = (bf16[32,4096]{1,0:T(8,128)(2,1)S(1)}, bf16[32,4096]{1,0:T(8,128)(2,1)S(1)}, u32[]{:S(2)}, u32[]{:S(2)}) collective-permute-start(bf16[32,4096]{1,0:T(8,128)(2,1)S(1)} %get-tuple-element.44), channel_id=1, source_target_pairs={{0,4},{1,5},{2,6},{3,7},{4,0},{5,1},{6,2},{7,3},{8,12},{9,13},{10,... | collective-permute-start | bytes 786440 | tf_op jit(solution)/shard_map/ppermute | solution.py:297
  108.7 2.5 %collective-permute-start.3 = (bf16[32,4096]{1,0:T(8,128)(2,1)S(1)}, bf16[32,4096]{1,0:T(8,128)(2,1)S(1)}, u32[]{:S(2)}, u32[]{:S(2)}) collective-permute-start(bf16[32,4096]{1,0:T(8,128)(2,1)S(1)} %get-tuple-element.43), channel_id=1, source_target_pairs={{0,6},{1,7},{2,0},{3,1},{4,2},{5,3},{6,4},{7,5},{8,14},{9,15},{10,... | collective-permute-start | bytes 786440 | tf_op jit(solution)/shard_map/ppermute | solution.py:297
  111.3 10.3 %collective-permute-done.1.r1 = bf16[32,4096]{1,0:T(8,128)(2,1)S(1)} collective-permute-done((bf16[32,4096]{1,0:T(8,128)(2,1)S(1)}, bf16[32,4096]{1,0:T(8,128)(2,1)S(1)}, u32[]{:S(2)}, u32[]{:S(2)}) %collective-permute-start.1) | collective-permute-done | bytes 262176 | tf_op jit(solution)/shard_map/ppermute | solution.py:297
  121.6 0.6 collective-permute-done.3.r3
  122.2 0.8 chain_ends.1
  123.0 0.3 collective-permute-start.4
  123.2 2.1 %collective-permute-start.5 = (bf16[96,128]{1,0:T(8,128)(2,1)S(1)}, bf16[96,128]{1,0:T(8,128)(2,1)S(1)}, u32[]{:S(2)}, u32[]{:S(2)}) collective-permute-start(bf16[96,128]{1,0:T(8,128)(2,1)S(1)} %get-tuple-element.31.pay), channel_id=1, source_target_pairs={{0,16},{8,24},{16,0},{24,8},{32,48},{40,56},{48,32},{56,40},{64,80... | collective-permute-start | bytes 73736 | tf_op jit(solution)/shard_map/ppermute | solution.py:305
  125.3 1.9 collective-permute-start.6
  127.2 0.9 collective-permute-done.4.r1
  128.1 0.5 collective-permute-done.5.r2
  128.6 0.6 collective-permute-done.6.r3
  129.2 0.6 cross.1
  129.8 1.2 collective-permute-start.7
  131.0 2.5 %collective-permute-start.8 = (bf16[96,128]{1,0:T(8,128)(2,1)S(1)}, bf16[96,128]{1,0:T(8,128)(2,1)S(1)}, u32[]{:S(2)}, u32[]{:S(2)}) collective-permute-start(bf16[96,128]{1,0:T(8,128)(2,1)S(1)} %get-tuple-element.34.pay), channel_id=1, source_target_pairs={{0,64},{8,72},{16,80},{24,88},{32,96},{40,104},{48,112},{56,120},{... | collective-permute-start | bytes 73736 | tf_op jit(solution)/shard_map/ppermute | solution.py:309
  133.5 0.9 collective-permute-start.9
  134.4 0.5 collective-permute-done.7.r1
  134.9 1.4 collective-permute-done.8.r2
  136.3 1.0 collective-permute-done.9.r3
  137.3 1.5 precision.1.refs_0_
  138.8 1.8 collective-permute-start.10
  140.5 2.4 %collective-permute-start.11 = (bf16[32,4096]{1,0:T(8,128)(2,1)S(1)}, bf16[32,4096]{1,0:T(8,128)(2,1)S(1)}, u32[]{:S(2)}, u32[]{:S(2)}) collective-permute-start(bf16[32,4096]{1,0:T(8,128)(2,1)S(1)} %precision.1.refs_0_), channel_id=1, source_target_pairs={{0,4},{1,5},{2,6},{3,7},{4,0},{5,1},{6,2},{7,3},{8,12},{9,13},{10,... | collective-permute-start | bytes 786440 | tf_op jit(solution)/shard_map/ppermute | solution.py:297
  142.9 1.0 collective-permute-start.12
  143.9 5.3 %collective-permute-done.10.refs_1_ = bf16[32,4096]{1,0:T(8,128)(2,1)S(1)} collective-permute-done((bf16[32,4096]{1,0:T(8,128)(2,1)S(1)}, bf16[32,4096]{1,0:T(8,128)(2,1)S(1)}, u32[]{:S(2)}, u32[]{:S(2)}) %collective-permute-start.10) | collective-permute-done | bytes 262176 | tf_op jit(solution)/shard_map/ppermute | solution.py:297
  149.2 2.9 %collective-permute-done.11.refs_2_ = bf16[32,4096]{1,0:T(8,128)(2,1)S(1)} collective-permute-done((bf16[32,4096]{1,0:T(8,128)(2,1)S(1)}, bf16[32,4096]{1,0:T(8,128)(2,1)S(1)}, u32[]{:S(2)}, u32[]{:S(2)}) %collective-permute-start.11) | collective-permute-done | bytes 262176 | tf_op jit(solution)/shard_map/ppermute | solution.py:297
  152.1 0.5 collective-permute-start.16
  152.6 1.0 collective-permute-done.15.refs_6_
  153.6 0.4 collective-permute-done.16.refs_7_
  154.0 5.6 %adjoint_x.1 = (f32[4,16,1024]{2,1,0:T(8,128)S(1)}, bf16[4,16,1024]{2,1,0:T(8,128)(2,1)S(1)}, bf16[4,16,1024]{2,1,0:T(8,128)(2,1)S(1)}, bf16[4,16,1024]{2,1,0:T(8,128)(2,1)S(1)}) custom-call(s32[4]{0:T(128)S(1)} %pad_add_fusion.idx, bf16[32,4096]{1,0:T(8,128)(2,1)S(1)} %precision.1.refs_0_, bf16[32,4096]{1,0:T(8,128)(2,1)S(1)} %collective-permute-done.10.refs_1_, ...), custom_call_target="tpu_custom_call" | custom-call | flops 2147483648 | bytes 8388608 | tf_op jit(solution)/shard_map/adjoint_x/pallas_call | solution.py:274
  159.6 0.6 collective-permute-start.17
  160.2 3.5 %collective-permute-start.18 = (bf16[4,16,1024]{2,1,0:T(8,128)(2,1)S(1)}, bf16[4,16,1024]{2,1,0:T(8,128)(2,1)S(1)}, u32[]{:S(2)}, u32[]{:S(2)}) collective-permute-start(bf16[4,16,1024]{2,1,0:T(8,128)(2,1)S(1)} %get-tuple-element.37), channel_id=1, source_target_pairs={{0,16},{8,24},{16,0},{24,8},{32,48},{40,56},{48,32},{56,40},{64,80... | collective-permute-start | bytes 393224 | tf_op jit(solution)/shard_map/ppermute | solution.py:305
  163.7 0.2 collective-permute-start.19
  163.8 5.6 %adjoint_z.1 = (f32[4,16,1024]{2,1,0:T(8,128)S(1)}, bf16[4,16,1024]{2,1,0:T(8,128)(2,1)S(1)}, bf16[4,16,1024]{2,1,0:T(8,128)(2,1)S(1)}, bf16[4,16,1024]{2,1,0:T(8,128)(2,1)S(1)}) custom-call(s32[4]{0:T(128)S(1)} %pad_add_fusion.idx, bf16[32,4096]{1,0:T(8,128)(2,1)S(1)} %precision.1.refs_0_, bf16[32,4096]{1,0:T(8,128)(2,1)S(1)} %collective-permute-done.10.refs_1_, ...), custom_call_target="tpu_custom_call" | custom-call | flops 2147483648 | bytes 8388608 | tf_op jit(solution)/shard_map/adjoint_z/pallas_call | solution.py:274
  169.4 0.7 collective-permute-start.23
  170.1 2.8 %collective-permute-start.24 = (bf16[4,16,1024]{2,1,0:T(8,128)(2,1)S(1)}, bf16[4,16,1024]{2,1,0:T(8,128)(2,1)S(1)}, u32[]{:S(2)}, u32[]{:S(2)}) collective-permute-start(bf16[4,16,1024]{2,1,0:T(8,128)(2,1)S(1)} %get-tuple-element.41), channel_id=1, source_target_pairs={{0,64},{8,72},{16,80},{24,88},{32,96},{40,104},{48,112},{56,120},{... | collective-permute-start | bytes 393224 | tf_op jit(solution)/shard_map/ppermute | solution.py:309
  172.9 0.9 collective-permute-start.25
  173.9 1.2 collective-permute-start.20
  175.1 0.9 collective-permute-start.21
  175.9 1.3 collective-permute-done.23
  177.2 1.2 collective-permute-start.22
  178.5 1.6 collective-permute-done.24
  180.1 0.2 collective-permute-done.25
  180.4 1.8 collective-permute-start.26
  182.2 0.5 collective-permute-start.27
  182.8 2.4 %collective-permute-start.28 = (f32[16,1024]{1,0:T(8,128)S(1)}, f32[16,1024]{1,0:T(8,128)S(1)}, u32[]{:S(2)}, u32[]{:S(2)}) collective-permute-start(f32[16,1024]{1,0:T(8,128)S(1)} %get-tuple-element.50), channel_id=1, source_target_pairs={{0,24},{8,0},{16,8},{24,16},{32,56},{40,32},{48,40},{56,48},{64,88... | collective-permute-start | bytes 196616 | tf_op jit(solution)/shard_map/ppermute | solution.py:305
  185.2 0.7 collective-permute-done.26
  186.0 2.0 %collective-permute-done.27 = f32[16,1024]{1,0:T(8,128)S(1)} collective-permute-done((f32[16,1024]{1,0:T(8,128)S(1)}, f32[16,1024]{1,0:T(8,128)S(1)}, u32[]{:S(2)}, u32[]{:S(2)}) %collective-permute-start.27) | collective-permute-done | bytes 65568 | tf_op jit(solution)/shard_map/ppermute | solution.py:305
  188.0 0.7 pad_maximum_fusion
  (34 shorter events, 0.4 us)
Async XLA Ops:
  1.0 5.8 %copy-start = (bf16[4096,2048]{1,0:T(8,128)(2,1)S(1)}, bf16[4096,2048]{1,0:T(8,128)(2,1)}, u32[]{:S(2)}) copy-start(bf16[4096,2048]{1,0:T(8,128)(2,1)} %refs_8_.3) | copy-start | bytes 50331652
  6.8 1.2 copy-start.3
  8.0 79.8 %copy-start.4 = (s32[512]{0:T(512)S(1)}, s32[512]{0:T(512)}, u32[]{:S(2)}) copy-start(s32[512]{0:T(512)} %param.9) | copy-start | bytes 6148
  16.0 1.3 copy-start.1
  17.3 86.9 %collective-permute-start = (f32[128,4096]{1,0:T(8,128)}, f32[128,4096]{1,0:T(8,128)}, u32[]{:S(2)}, u32[]{:S(2)}) collective-permute-start(f32[128,4096]{1,0:T(8,128)} %get-tuple-element.25), channel_id=1, source_target_pairs={{0,1},{1,0},{2,3},{3,2},{4,5},{5,4},{6,7},{7,6},{8,9},{9,8},{10,11... | collective-permute-start | bytes 6291464 | tf_op jit(solution)/shard_map/ppermute | solution.py:301
  99.7 4.5 %copy-start.2 = (f32[128,4096]{1,0:T(8,128)S(1)}, f32[128,4096]{1,0:T(8,128)}, u32[]{:S(2)}) copy-start(f32[128,4096]{1,0:T(8,128)} %copy-done.1) | copy-start | bytes 6291460
  106.2 15.4 %collective-permute-start.1 = (bf16[32,4096]{1,0:T(8,128)(2,1)S(1)}, bf16[32,4096]{1,0:T(8,128)(2,1)S(1)}, u32[]{:S(2)}, u32[]{:S(2)}) collective-permute-start(bf16[32,4096]{1,0:T(8,128)(2,1)S(1)} %get-tuple-element.45), channel_id=1, source_target_pairs={{0,2},{1,3},{2,4},{3,5},{4,6},{5,7},{6,0},{7,1},{8,10},{9,11},{10,... | collective-permute-start | bytes 786440 | tf_op jit(solution)/shard_map/ppermute | solution.py:297
  106.2 15.3 %collective-permute-start.2 = (bf16[32,4096]{1,0:T(8,128)(2,1)S(1)}, bf16[32,4096]{1,0:T(8,128)(2,1)S(1)}, u32[]{:S(2)}, u32[]{:S(2)}) collective-permute-start(bf16[32,4096]{1,0:T(8,128)(2,1)S(1)} %get-tuple-element.44), channel_id=1, source_target_pairs={{0,4},{1,5},{2,6},{3,7},{4,0},{5,1},{6,2},{7,3},{8,12},{9,13},{10,... | collective-permute-start | bytes 786440 | tf_op jit(solution)/shard_map/ppermute | solution.py:297
  108.7 13.5 %collective-permute-start.3 = (bf16[32,4096]{1,0:T(8,128)(2,1)S(1)}, bf16[32,4096]{1,0:T(8,128)(2,1)S(1)}, u32[]{:S(2)}, u32[]{:S(2)}) collective-permute-start(bf16[32,4096]{1,0:T(8,128)(2,1)S(1)} %get-tuple-element.43), channel_id=1, source_target_pairs={{0,6},{1,7},{2,0},{3,1},{4,2},{5,3},{6,4},{7,5},{8,14},{9,15},{10,... | collective-permute-start | bytes 786440 | tf_op jit(solution)/shard_map/ppermute | solution.py:297
  123.0 5.1 %collective-permute-start.4 = (bf16[96,128]{1,0:T(8,128)(2,1)S(1)}, bf16[96,128]{1,0:T(8,128)(2,1)S(1)}, u32[]{:S(2)}, u32[]{:S(2)}) collective-permute-start(bf16[96,128]{1,0:T(8,128)(2,1)S(1)} %get-tuple-element.31.pay), channel_id=1, source_target_pairs={{0,8},{8,16},{16,24},{24,0},{32,40},{40,48},{48,56},{56,32},{64,72... | collective-permute-start | bytes 73736 | tf_op jit(solution)/shard_map/ppermute | solution.py:305
  123.2 5.3 %collective-permute-start.5 = (bf16[96,128]{1,0:T(8,128)(2,1)S(1)}, bf16[96,128]{1,0:T(8,128)(2,1)S(1)}, u32[]{:S(2)}, u32[]{:S(2)}) collective-permute-start(bf16[96,128]{1,0:T(8,128)(2,1)S(1)} %get-tuple-element.31.pay), channel_id=1, source_target_pairs={{0,16},{8,24},{16,0},{24,8},{32,48},{40,56},{48,32},{56,40},{64,80... | collective-permute-start | bytes 73736 | tf_op jit(solution)/shard_map/ppermute | solution.py:305
  125.3 3.9 %collective-permute-start.6 = (bf16[96,128]{1,0:T(8,128)(2,1)S(1)}, bf16[96,128]{1,0:T(8,128)(2,1)S(1)}, u32[]{:S(2)}, u32[]{:S(2)}) collective-permute-start(bf16[96,128]{1,0:T(8,128)(2,1)S(1)} %get-tuple-element.31.pay), channel_id=1, source_target_pairs={{0,24},{8,0},{16,8},{24,16},{32,56},{40,32},{48,40},{56,48},{64,88... | collective-permute-start | bytes 73736 | tf_op jit(solution)/shard_map/ppermute | solution.py:305
  129.8 5.1 %collective-permute-start.7 = (bf16[96,128]{1,0:T(8,128)(2,1)S(1)}, bf16[96,128]{1,0:T(8,128)(2,1)S(1)}, u32[]{:S(2)}, u32[]{:S(2)}) collective-permute-start(bf16[96,128]{1,0:T(8,128)(2,1)S(1)} %get-tuple-element.34.pay), channel_id=1, source_target_pairs={{0,32},{8,40},{16,48},{24,56},{32,64},{40,72},{48,80},{56,88},{64,... | collective-permute-start | bytes 73736 | tf_op jit(solution)/shard_map/ppermute | solution.py:309
  131.0 5.3 %collective-permute-start.8 = (bf16[96,128]{1,0:T(8,128)(2,1)S(1)}, bf16[96,128]{1,0:T(8,128)(2,1)S(1)}, u32[]{:S(2)}, u32[]{:S(2)}) collective-permute-start(bf16[96,128]{1,0:T(8,128)(2,1)S(1)} %get-tuple-element.34.pay), channel_id=1, source_target_pairs={{0,64},{8,72},{16,80},{24,88},{32,96},{40,104},{48,112},{56,120},{... | collective-permute-start | bytes 73736 | tf_op jit(solution)/shard_map/ppermute | solution.py:309
  133.5 3.8 %collective-permute-start.9 = (bf16[96,128]{1,0:T(8,128)(2,1)S(1)}, bf16[96,128]{1,0:T(8,128)(2,1)S(1)}, u32[]{:S(2)}, u32[]{:S(2)}) collective-permute-start(bf16[96,128]{1,0:T(8,128)(2,1)S(1)} %get-tuple-element.34.pay), channel_id=1, source_target_pairs={{0,96},{8,104},{16,112},{24,120},{32,0},{40,8},{48,16},{56,24},{64... | collective-permute-start | bytes 73736 | tf_op jit(solution)/shard_map/ppermute | solution.py:309
  138.8 10.5 %collective-permute-start.10 = (bf16[32,4096]{1,0:T(8,128)(2,1)S(1)}, bf16[32,4096]{1,0:T(8,128)(2,1)S(1)}, u32[]{:S(2)}, u32[]{:S(2)}) collective-permute-start(bf16[32,4096]{1,0:T(8,128)(2,1)S(1)} %precision.1.refs_0_), channel_id=1, source_target_pairs={{0,2},{1,3},{2,4},{3,5},{4,6},{5,7},{6,0},{7,1},{8,10},{9,11},{10,... | collective-permute-start | bytes 786440 | tf_op jit(solution)/shard_map/ppermute | solution.py:297
  140.5 11.6 %collective-permute-start.11 = (bf16[32,4096]{1,0:T(8,128)(2,1)S(1)}, bf16[32,4096]{1,0:T(8,128)(2,1)S(1)}, u32[]{:S(2)}, u32[]{:S(2)}) collective-permute-start(bf16[32,4096]{1,0:T(8,128)(2,1)S(1)} %precision.1.refs_0_), channel_id=1, source_target_pairs={{0,4},{1,5},{2,6},{3,7},{4,0},{5,1},{6,2},{7,3},{8,12},{9,13},{10,... | collective-permute-start | bytes 786440 | tf_op jit(solution)/shard_map/ppermute | solution.py:297
  142.9 9.2 %collective-permute-start.12 = (bf16[32,4096]{1,0:T(8,128)(2,1)S(1)}, bf16[32,4096]{1,0:T(8,128)(2,1)S(1)}, u32[]{:S(2)}, u32[]{:S(2)}) collective-permute-start(bf16[32,4096]{1,0:T(8,128)(2,1)S(1)} %precision.1.refs_0_), channel_id=1, source_target_pairs={{0,6},{1,7},{2,0},{3,1},{4,2},{5,3},{6,4},{7,5},{8,14},{9,15},{10,... | collective-permute-start | bytes 786440 | tf_op jit(solution)/shard_map/ppermute | solution.py:297
  143.9 8.7 %collective-permute-start.13 = (bf16[32,4096]{1,0:T(8,128)(2,1)S(1)}, bf16[32,4096]{1,0:T(8,128)(2,1)S(1)}, u32[]{:S(2)}, u32[]{:S(2)}) collective-permute-start(bf16[32,4096]{1,0:T(8,128)(2,1)S(1)} %precision.1.refs_0_), channel_id=1, source_target_pairs={{0,1},{1,0},{2,3},{3,2},{4,5},{5,4},{6,7},{7,6},{8,9},{9,8},{10,11... | collective-permute-start | bytes 786440 | tf_op jit(solution)/shard_map/ppermute | solution.py:301
  149.2 3.4 %collective-permute-start.14 = (bf16[32,4096]{1,0:T(8,128)(2,1)S(1)}, bf16[32,4096]{1,0:T(8,128)(2,1)S(1)}, u32[]{:S(2)}, u32[]{:S(2)}) collective-permute-start(bf16[32,4096]{1,0:T(8,128)(2,1)S(1)} %collective-permute-done.10.refs_1_), channel_id=1, source_target_pairs={{0,1},{1,0},{2,3},{3,2},{4,5},{5,4},{6,7},{7,6},{8,9},{9,8},{10,11... | collective-permute-start | bytes 786440 | tf_op jit(solution)/shard_map/ppermute | solution.py:301
  152.1 1.5 collective-permute-start.15
  152.1 1.9 %collective-permute-start.16 = (bf16[32,4096]{1,0:T(8,128)(2,1)S(1)}, bf16[32,4096]{1,0:T(8,128)(2,1)S(1)}, u32[]{:S(2)}, u32[]{:S(2)}) collective-permute-start(bf16[32,4096]{1,0:T(8,128)(2,1)S(1)} %collective-permute-done.12.refs_3_), channel_id=1, source_target_pairs={{0,1},{1,0},{2,3},{3,2},{4,5},{5,4},{6,7},{7,6},{8,9},{9,8},{10,11... | collective-permute-start | bytes 786440 | tf_op jit(solution)/shard_map/ppermute | solution.py:301
  159.6 13.3 %collective-permute-start.17 = (bf16[4,16,1024]{2,1,0:T(8,128)(2,1)S(1)}, bf16[4,16,1024]{2,1,0:T(8,128)(2,1)S(1)}, u32[]{:S(2)}, u32[]{:S(2)}) collective-permute-start(bf16[4,16,1024]{2,1,0:T(8,128)(2,1)S(1)} %get-tuple-element.36), channel_id=1, source_target_pairs={{0,8},{8,16},{16,24},{24,0},{32,40},{40,48},{48,56},{56,32},{64,72... | collective-permute-start | bytes 393224 | tf_op jit(solution)/shard_map/ppermute | solution.py:305
  160.2 13.6 %collective-permute-start.18 = (bf16[4,16,1024]{2,1,0:T(8,128)(2,1)S(1)}, bf16[4,16,1024]{2,1,0:T(8,128)(2,1)S(1)}, u32[]{:S(2)}, u32[]{:S(2)}) collective-permute-start(bf16[4,16,1024]{2,1,0:T(8,128)(2,1)S(1)} %get-tuple-element.37), channel_id=1, source_target_pairs={{0,16},{8,24},{16,0},{24,8},{32,48},{40,56},{48,32},{56,40},{64,80... | collective-permute-start | bytes 393224 | tf_op jit(solution)/shard_map/ppermute | solution.py:305
  163.7 10.2 %collective-permute-start.19 = (bf16[4,16,1024]{2,1,0:T(8,128)(2,1)S(1)}, bf16[4,16,1024]{2,1,0:T(8,128)(2,1)S(1)}, u32[]{:S(2)}, u32[]{:S(2)}) collective-permute-start(bf16[4,16,1024]{2,1,0:T(8,128)(2,1)S(1)} %get-tuple-element.38), channel_id=1, source_target_pairs={{0,24},{8,0},{16,8},{24,16},{32,56},{40,32},{48,40},{56,48},{64,88... | collective-permute-start | bytes 393224 | tf_op jit(solution)/shard_map/ppermute | solution.py:305
  169.4 7.8 %collective-permute-start.23 = (bf16[4,16,1024]{2,1,0:T(8,128)(2,1)S(1)}, bf16[4,16,1024]{2,1,0:T(8,128)(2,1)S(1)}, u32[]{:S(2)}, u32[]{:S(2)}) collective-permute-start(bf16[4,16,1024]{2,1,0:T(8,128)(2,1)S(1)} %get-tuple-element.40), channel_id=1, source_target_pairs={{0,32},{8,40},{16,48},{24,56},{32,64},{40,72},{48,80},{56,88},{64,... | collective-permute-start | bytes 393224 | tf_op jit(solution)/shard_map/ppermute | solution.py:309
  170.1 10.0 %collective-permute-start.24 = (bf16[4,16,1024]{2,1,0:T(8,128)(2,1)S(1)}, bf16[4,16,1024]{2,1,0:T(8,128)(2,1)S(1)}, u32[]{:S(2)}, u32[]{:S(2)}) collective-permute-start(bf16[4,16,1024]{2,1,0:T(8,128)(2,1)S(1)} %get-tuple-element.41), channel_id=1, source_target_pairs={{0,64},{8,72},{16,80},{24,88},{32,96},{40,104},{48,112},{56,120},{... | collective-permute-start | bytes 393224 | tf_op jit(solution)/shard_map/ppermute | solution.py:309
  172.9 7.5 %collective-permute-start.25 = (bf16[4,16,1024]{2,1,0:T(8,128)(2,1)S(1)}, bf16[4,16,1024]{2,1,0:T(8,128)(2,1)S(1)}, u32[]{:S(2)}, u32[]{:S(2)}) collective-permute-start(bf16[4,16,1024]{2,1,0:T(8,128)(2,1)S(1)} %get-tuple-element.42), channel_id=1, source_target_pairs={{0,96},{8,104},{16,112},{24,120},{32,0},{40,8},{48,16},{56,24},{64... | collective-permute-start | bytes 393224 | tf_op jit(solution)/shard_map/ppermute | solution.py:309
  173.9 8.9 %collective-permute-start.20 = (f32[16,1024]{1,0:T(8,128)S(1)}, f32[16,1024]{1,0:T(8,128)S(1)}, u32[]{:S(2)}, u32[]{:S(2)}) collective-permute-start(f32[16,1024]{1,0:T(8,128)S(1)} %get-tuple-element.46), channel_id=1, source_target_pairs={{0,32},{8,40},{16,48},{24,56},{32,64},{40,72},{48,80},{56,88},{64,... | collective-permute-start | bytes 196616 | tf_op jit(solution)/shard_map/ppermute | solution.py:309
  175.1 10.2 %collective-permute-start.21 = (f32[16,1024]{1,0:T(8,128)S(1)}, f32[16,1024]{1,0:T(8,128)S(1)}, u32[]{:S(2)}, u32[]{:S(2)}) collective-permute-start(f32[16,1024]{1,0:T(8,128)S(1)} %get-tuple-element.48), channel_id=1, source_target_pairs={{0,64},{8,72},{16,80},{24,88},{32,96},{40,104},{48,112},{56,120},{... | collective-permute-start | bytes 196616 | tf_op jit(solution)/shard_map/ppermute | solution.py:309
  177.2 8.0 %collective-permute-start.22 = (f32[16,1024]{1,0:T(8,128)S(1)}, f32[16,1024]{1,0:T(8,128)S(1)}, u32[]{:S(2)}, u32[]{:S(2)}) collective-permute-start(f32[16,1024]{1,0:T(8,128)S(1)} %get-tuple-element.47), channel_id=1, source_target_pairs={{0,96},{8,104},{16,112},{24,120},{32,0},{40,8},{48,16},{56,24},{64... | collective-permute-start | bytes 196616 | tf_op jit(solution)/shard_map/ppermute | solution.py:309
  180.4 5.5 %collective-permute-start.26 = (f32[16,1024]{1,0:T(8,128)S(1)}, f32[16,1024]{1,0:T(8,128)S(1)}, u32[]{:S(2)}, u32[]{:S(2)}) collective-permute-start(f32[16,1024]{1,0:T(8,128)S(1)} %get-tuple-element.49), channel_id=1, source_target_pairs={{0,8},{8,16},{16,24},{24,0},{32,40},{40,48},{48,56},{56,32},{64,72... | collective-permute-start | bytes 196616 | tf_op jit(solution)/shard_map/ppermute | solution.py:305
  182.2 5.8 %collective-permute-start.27 = (f32[16,1024]{1,0:T(8,128)S(1)}, f32[16,1024]{1,0:T(8,128)S(1)}, u32[]{:S(2)}, u32[]{:S(2)}) collective-permute-start(f32[16,1024]{1,0:T(8,128)S(1)} %get-tuple-element.51), channel_id=1, source_target_pairs={{0,16},{8,24},{16,0},{24,8},{32,48},{40,56},{48,32},{56,40},{64,80... | collective-permute-start | bytes 196616 | tf_op jit(solution)/shard_map/ppermute | solution.py:305
  182.8 5.2 %collective-permute-start.28 = (f32[16,1024]{1,0:T(8,128)S(1)}, f32[16,1024]{1,0:T(8,128)S(1)}, u32[]{:S(2)}, u32[]{:S(2)}) collective-permute-start(f32[16,1024]{1,0:T(8,128)S(1)} %get-tuple-element.50), channel_id=1, source_target_pairs={{0,24},{8,0},{16,8},{24,16},{32,56},{40,32},{48,40},{56,48},{64,88... | collective-permute-start | bytes 196616 | tf_op jit(solution)/shard_map/ppermute | solution.py:305

commit v2 on v0

v2 whole, which is shorter than its diff:
```python
import functools

import jax
import jax.numpy as jnp
from jax import lax
from jax.experimental import pallas as pl
from jax.experimental.pallas import tpu as pltpu
from jax.sharding import PartitionSpec as P

BLK = 128
CH = 256
AUG = 48
COLS = 32
BF = jnp.bfloat16
F32 = jnp.float32
NT = (((1,), (1,)), ((), ()))
TN = (((0,), (0,)), ((), ()))
MB = 1 << 20
VMEM = pl.BlockSpec(memory_space=pltpu.VMEM)
SMEM = pl.BlockSpec(memory_space=pltpu.SMEM)
HBM = pl.BlockSpec(memory_space=pltpu.HBM)


def shape(dims, dtype):
    return jax.ShapeDtypeStruct(dims, dtype)


def call(kernel, name, out_shape, in_specs, args, scratch=(), mib=16, flops=0, data=0, after=()):
    single = not isinstance(out_shape, list)
    n, m = len(args), len(after)

    def body(*refs):
        kernel(*refs[:n], *refs[n + m :])

    return pl.pallas_call(
        body,
        out_shape=out_shape,
        in_specs=in_specs + [pl.BlockSpec(memory_space=pl.ANY)] * m,
        out_specs=VMEM if single else [VMEM] * len(out_shape),
        scratch_shapes=list(scratch),
        compiler_params=pltpu.CompilerParams(vmem_limit_bytes=mib * MB),
        cost_estimate=pl.CostEstimate(flops=flops, bytes_accessed=data, transcendentals=0),
        name=name,
    )(*args, *after)


def hbm(v):
    return pltpu.with_memory_space_constraint(v, pltpu.HBM)


def fetch(green, start, buf, sem, i):
    tile = buf.shape[0] // sem.shape[0]
    return pltpu.make_async_copy(
        green.at[pl.ds(start + i * tile, tile), :], buf.at[pl.ds(i * tile, tile), :], sem.at[i]
    )


def expand(blocks, gate):
    n, wide = blocks.shape[0], gate.shape[1]
    mine = lax.broadcasted_iota(jnp.int32, (n, wide), 1) // BLK
    pick = jnp.where(mine == lax.broadcasted_iota(jnp.int32, (n, wide), 0), 1.0, 0.0).astype(BF)
    gate[...] = lax.dot_general(
        blocks[...].astype(F32).astype(BF), pick, TN, preferred_element_type=F32
    )


def mask_rows(buf, gate, i, tile, first):
    for r in range(i * tile // BLK, (i + 1) * tile // BLK):
        at = slice(r * BLK, (r + 1) * BLK)
        buf[at, :] = buf[at, :] * gate[first + r : first + r + 1, :].astype(BF)


def forward_kernel(idx, green, blocks, probes, mine, send, buf, own_blocks, own_probes, panel, gate, sem, sem2):
    core = idx[0]
    steps = sem.shape[0]
    tile = buf.shape[0] // steps
    small = [
        pltpu.make_async_copy(blocks, own_blocks, sem2.at[0]),
        pltpu.make_async_copy(probes, own_probes, sem2.at[1]),
    ]
    for copy in small:
        copy.start()
    for i in range(3):
        fetch(green, 0, buf, sem, i).start()
    small[0].wait()
    expand(own_blocks, gate)
    small[1].wait()
    for part in range(2):
        at = pl.multiple_of(lax.rem(part + core, 2) * 128, 128)
        panel[pl.ds(at, 128), :] = own_probes[:, part * 128 : (part + 1) * 128].T
    for i in range(steps):
        fetch(green, 0, buf, sem, i).wait()
        if i + 3 < steps:
            fetch(green, 0, buf, sem, i + 3).start()
        mask_rows(buf, gate, i, tile, 0)
        at = slice(i * tile, (i + 1) * tile)
        part = lax.dot_general(panel[...], buf[at, :], NT, preferred_element_type=F32)
        mine[:, at] = part[:128, :]
        send[:, at] = part[128:, :]


def forward(idx, green, blocks, probes, after=()):
    rows, par_dev = green.shape
    return call(
        forward_kernel,
        "forward",
        [shape((128, rows), F32)] * 2,
        [SMEM, HBM, HBM, HBM],
        (idx, hbm(green), hbm(blocks), hbm(probes)),
        [
            pltpu.VMEM((rows, par_dev), BF),
            pltpu.VMEM(blocks.shape, jnp.int32),
            pltpu.VMEM(probes.shape, BF),
            pltpu.VMEM((256, par_dev), BF),
            pltpu.VMEM((rows // BLK, par_dev), F32),
            pltpu.SemaphoreType.DMA((8,)),
            pltpu.SemaphoreType.DMA((2,)),
        ],
        flops=2 * rows * par_dev * 256,
        data=2 * rows * par_dev,
        mib=32,
        after=after,
    )


def core_sum_kernel(idx, mine, peer, own, s1, s2, s3):
    y = idx[1]
    for k, ref in enumerate((own, s1, s2, s3)):
        at = pl.ds(pl.multiple_of(lax.rem(y + k, 4) * COLS, COLS), COLS)
        ref[...] = (mine[at, :] + peer[at, :]).astype(ref.dtype)


def core_sum(idx, mine, peer, after=()):
    rows = mine.shape[1]
    return call(
        core_sum_kernel,
        "core_sum",
        [shape((COLS, rows), F32)] + [shape((COLS, rows), BF)] * 3,
        [SMEM] + [VMEM] * 2,
        (idx, mine, peer),
        after=after,
    )


def info_kernel(idx, stations, decay, noise_scale, out):
    slot = idx[3] * 32 + idx[2] * 8 + idx[1] * 2 + idx[0]
    lane = lax.broadcasted_iota(jnp.int32, (1, 128), 1)
    rows = [
        stations[...].astype(F32),
        jnp.where(lane == slot, decay[0, 0], 0.0),
        jnp.where(lane == slot, noise_scale[0, 0], 0.0),
        jnp.zeros((2, 128), F32),
    ]
    out[...] = jnp.broadcast_to(jnp.concatenate(rows, axis=0)[None], out.shape)


def info(idx, stations, decay, noise_scale):
    return call(
        info_kernel,
        "info",
        shape((8, 8, 128), F32),
        [SMEM, VMEM, SMEM, SMEM],
        (idx, stations.reshape(4, 128), decay.reshape(1, 1), noise_scale.reshape(1, 1)),
    )


def params_kernel(table, sums):
    sums[...] = jnp.broadcast_to(jnp.sum(table[...], axis=0)[None], sums.shape)


def chain_kernel(table, near, ends, tops, hits):
    held = []
    here = lax.broadcasted_iota(jnp.int32, (CH, CH), 0)
    there = lax.broadcasted_iota(jnp.int32, (CH, CH), 1)
    sid = lax.broadcasted_iota(jnp.int32, (128, CH), 0).astype(F32)
    for b in range(hits.shape[1] // CH):
        at = slice(b * CH, (b + 1) * CH)
        r = (b % 2) * 2
        got = table[b // 2]
        row = jnp.concatenate([got[r : r + 1, :], got[r + 1 : r + 2, :]], axis=1)
        hit = jnp.broadcast_to(row, (128, CH)) == sid
        hit16 = jnp.where(hit, 1.0, 0.0).astype(BF)
        hits[:, at] = hit16
        same = lax.dot_general(hit16, hit16, TN, preferred_element_type=F32) > 0.5
        prior = jnp.max(jnp.where(same & (here < there), here, -1), axis=0, keepdims=True)
        later = jnp.min(jnp.where(same & (here > there), here, CH), axis=0, keepdims=True)
        near[b] = jnp.where((here == prior) | (here == later), 1.0, 0.0).astype(BF)
        ends[:128, at] = jnp.where(hit & (prior < 0), 1.0, 0.0).astype(BF)
        ends[128:, at] = jnp.where(hit & (later >= CH), 1.0, 0.0).astype(BF)
        held.append(jnp.max(jnp.where(hit, 1.0, 0.0), axis=1, keepdims=True))
    n = len(held)
    before = jnp.zeros((128, 1), F32)
    after = jnp.zeros((128, 1), F32)
    for b in range(n):
        at = slice(b * CH, (b + 1) * CH)
        tops[:128, at] = (ends[:128, at].astype(F32) * (1.0 - before)).astype(BF)
        before = jnp.maximum(before, held[b])
        e = n - 1 - b
        at = slice(e * CH, (e + 1) * CH)
        tops[128:, at] = (ends[128:, at].astype(F32) * (1.0 - after)).astype(BF)
        after = jnp.maximum(after, held[e])


def chains(table, rows, after):
    n = rows // CH
    return call(
        chain_kernel,
        "chains",
        [shape((n, CH, CH), BF)] + [shape((256, rows), BF)] * 2 + [shape((128, rows), BF)],
        [VMEM],
        (table,),
        data=12 * MB,
        after=after,
    )


def coef_kernel(params, hits, coef, station):
    total = jnp.sum(params[...], axis=0)
    rate, level = total[4:5, :], total[5:6, :]
    scale = 1.0 / (level * level)
    rows = [(1.0 - rate * rate) * scale, rate * rate * scale, rate * scale]
    for i, row in enumerate(rows):
        station[i : i + 1, :] = row
    station[3:8, :] = jnp.zeros((5, 128), F32)
    split = []
    for row in rows:
        high = row.astype(BF)
        rest = row - high.astype(F32)
        mid = rest.astype(BF)
        split += [high, mid, (rest - mid.astype(F32)).astype(BF)]
    table = jnp.concatenate(split + [jnp.zeros((7, 128), BF)], axis=0)
    out = jnp.dot(table, hits[...], preferred_element_type=F32)
    for i in range(3):
        coef[i : i + 1, :] = out[3 * i : 3 * i + 1, :] + out[3 * i + 1 : 3 * i + 2, :] + out[3 * i + 2 : 3 * i + 3, :]
    coef[3:8, :] = jnp.zeros((5, coef.shape[1]), F32)


def coefs(params, hits):
    return call(
        coef_kernel,
        "coefs",
        [shape((8, hits.shape[1]), F32), shape((8, 128), F32)],
        [VMEM] * 2,
        (params, hits),
    )


def seen(v):
    return v[COLS : COLS + 1, :] > 0.5


def rows_kernel(own_h, r1_h, r2_h, r3_h, near_h, ends_h, coef, out, pay, *scratch):
    own, r1, r2, r3, near, ends, yaug, tips, carry, sem = scratch
    copies = [
        pltpu.make_async_copy(src, dst, sem.at[i])
        for i, (src, dst) in enumerate(
            ((own_h, own), (r1_h, r1), (r2_h, r2), (r3_h, r3), (ends_h, ends), (near_h, near))
        )
    ]
    for copy in copies:
        copy.start()
    for copy in copies[:4]:
        copy.wait()
    n = near.shape[0]
    total = own[...] + r1[...].astype(F32) + r2[...].astype(F32) + r3[...].astype(F32)
    yaug[:COLS, :] = total.astype(BF)
    yaug[COLS:, :] = jnp.ones((AUG - COLS, total.shape[1]), BF)
    copies[4].wait()
    spans = [slice(b * CH, (b + 1) * CH) for b in range(n)]
    for b in range(n):
        tips[b] = lax.dot_general(yaug[:, spans[b]], ends[:, spans[b]], NT, preferred_element_type=F32)
    below = jnp.zeros((AUG, 128), F32)
    above = jnp.zeros((AUG, 128), F32)
    for b in range(n):
        carry[b, :, :128] = below.astype(BF)
        here = tips[b, :, 128:]
        below = jnp.where(seen(here), here, below)
        e = n - 1 - b
        carry[e, :, 128:] = above.astype(BF)
        here = tips[e, :, :128]
        above = jnp.where(seen(here), here, above)
    tip = jnp.concatenate([above, below], axis=0).astype(BF)
    pay[...] = jnp.broadcast_to(tip[None], pay.shape)
    copies[5].wait()
    for b in range(n):
        y = yaug[:, spans[b]]
        around = jnp.dot(y, near[b], preferred_element_type=F32) + jnp.dot(
            carry[b], ends[:, spans[b]], preferred_element_type=F32
        )
        alpha = coef[0:1, spans[b]] + coef[1:2, spans[b]] * around[COLS : COLS + 1, :]
        out[:, spans[b]] = (
            alpha * y[:COLS, :].astype(F32) - coef[2:3, spans[b]] * around[:COLS, :]
        ).astype(BF)


def group_rows(own, recv, near, ends, coef):
    rows = own.shape[1]
    n = rows // CH
    return call(
        rows_kernel,
        "group_rows",
        [shape((COLS, rows), BF), shape((16, 2 * AUG, 128), BF)],
        [HBM] * 6 + [VMEM],
        (*map(hbm, (own, *recv, near, ends)), coef),
        [pltpu.VMEM((COLS, rows), F32)]
        + [pltpu.VMEM((COLS, rows), BF)] * 3
        + [pltpu.VMEM((n, CH, CH), BF), pltpu.VMEM((256, rows), BF)]
        + [pltpu.VMEM((AUG, rows), BF), pltpu.VMEM((n, AUG, 256), F32), pltpu.VMEM((n, AUG, 256), BF)]
        + [pltpu.SemaphoreType.DMA((6,))],
    )


def tie_kernel(idx, station, pay, out):
    me = idx[3] * 4 + idx[2]
    n = pay.shape[0]
    low = jnp.zeros((AUG, 128), F32)
    high = jnp.zeros((AUG, 128), F32)
    for j in range(n - 1):
        last = pay[j, AUG:, :].astype(F32)
        low = jnp.where(jnp.where(me > j, last[COLS : COLS + 1, :], 0.0) > 0.5, last, low)
        e = n - 1 - j
        first = pay[e, :AUG, :].astype(F32)
        high = jnp.where(jnp.where(me < e, first[COLS : COLS + 1, :], 0.0) > 0.5, first, high)
    square, rate = station[1:2, :], station[2:3, :]
    own = pay[me].astype(F32)
    for at, base, other in ((0, own[:AUG, :], low), (128, own[AUG:, :], high)):
        value = square * base[:COLS, :] - rate * other[:COLS, :]
        value = jnp.where(seen(base) & seen(other), value, 0.0).astype(BF)
        out[:, :, at : at + 128] = jnp.broadcast_to(value[None], (8, COLS, 128))


def tie(idx, station, pay, after):
    return call(
        tie_kernel, "tie", shape((8, COLS, 256), BF), [SMEM] + [VMEM] * 2, (idx, station, pay), after=after
    )


def panel_product(green, blocks, copies, panel, buf, own_blocks, acc, gate, sem, sem_blocks):
    steps = sem.shape[0]
    tile = buf.shape[0] // steps
    small = pltpu.make_async_copy(blocks, own_blocks, sem_blocks)
    small.start()
    for copy in copies:
        copy.start()
    for i in range(3):
        fetch(green, 0, buf, sem, i).start()
    small.wait()
    expand(own_blocks, gate)
    for copy in copies:
        copy.wait()
    for i in range(steps):
        fetch(green, 0, buf, sem, i).wait()
        if i + 3 < steps:
            fetch(green, 0, buf, sem, i + 3).start()
        mask_rows(buf, gate, i, tile, 0)
        at = slice(i * tile, (i + 1) * tile)
        part = jnp.dot(panel[:, at], buf[at, :], preferred_element_type=F32)
        acc[...] = part if i == 0 else acc[...] + part


def product_scratch(rows, par_dev, blocks):
    return [
        pltpu.VMEM((256, rows), BF),
        pltpu.VMEM((rows, par_dev), BF),
        pltpu.VMEM(blocks.shape, jnp.int32),
        pltpu.VMEM((256, par_dev), F32),
        pltpu.VMEM((rows // BLK, par_dev), F32),
        pltpu.SemaphoreType.DMA((8,)),
        pltpu.SemaphoreType.DMA((9,)),
    ]


def end_rows_kernel(green, blocks, tops, out, panel, buf, own_blocks, acc, gate, sem, sem2):
    copies = [pltpu.make_async_copy(tops, panel, sem2.at[0])]
    panel_product(green, blocks, copies, panel, buf, own_blocks, acc, gate, sem, sem2.at[8])
    out[...] = acc[...].astype(BF)


def end_rows(green, blocks, tops, after):
    rows, par_dev = green.shape
    return call(
        end_rows_kernel,
        "end_rows",
        shape((256, par_dev), BF),
        [HBM] * 3,
        tuple(map(hbm, (green, blocks, tops))),
        product_scratch(rows, par_dev, blocks),
        flops=2 * rows * par_dev * 256,
        data=2 * rows * par_dev,
        mib=32,
        after=after,
    )


def adjoint_kernel(idx, *refs):
    pieces, (green, blocks, out) = refs[:8], refs[8:11]
    panel, buf, own_blocks, acc, gate, sem, sem2 = refs[11:]
    core, y = idx[0], idx[1]
    copies = []
    for k in range(4):
        spot = lax.rem(y + 4 - k, 4) * COLS
        for base, j in ((core, k), (1 - core, 4 + k)):
            at = pl.ds(pl.multiple_of(base * 128 + spot, COLS), COLS)
            copies.append(pltpu.make_async_copy(pieces[j], panel.at[at, :], sem2.at[j]))
    panel_product(green, blocks, copies, panel, buf, own_blocks, acc, gate, sem, sem2.at[8])
    out[...] = acc[...]


def adjoint(idx, pieces, green, blocks, after=()):
    rows, par_dev = green.shape
    return call(
        adjoint_kernel,
        "adjoint",
        shape((256, par_dev), F32),
        [SMEM] + [HBM] * 10,
        (idx, *map(hbm, (*pieces, green, blocks))),
        product_scratch(rows, par_dev, blocks),
        flops=2 * rows * par_dev * 256,
        data=2 * rows * par_dev,
        mib=32,
        after=after,
    )


def finish_kernel(axis, idx, product, tied, rows_g, keep, s1, s2, s3, ties, acc):
    for p in range(8):
        at = (p % 2) * 128 + (p // 2) * COLS
        ties[at : at + COLS, :] = tied[p]
    wide = acc.shape[1]
    at = slice(0, wide) if axis == "x" else slice(wide, 2 * wide)
    acc[...] = product[:, at] + jnp.dot(ties[...], rows_g[:, at], preferred_element_type=F32)
    me = idx[2] if axis == "x" else idx[3]
    for k, ref in enumerate((keep, s1, s2, s3)):
        to = lax.rem(me + k, 4)
        for j in range(4):
            row = j * 64 + to * 16 if axis == "x" else to * 64 + j * 16
            ref[j] = acc[pl.ds(pl.multiple_of(row, 16), 16), :].astype(ref.dtype)


def finish(axis, idx, product, tied, rows_g, after=()):
    wide = product.shape[1] // 2
    return call(
        functools.partial(finish_kernel, axis),
        "finish_" + axis,
        [shape((4, 16, wide), F32)] + [shape((4, 16, wide), BF)] * 3,
        [SMEM] + [VMEM] * 3,
        (idx, product, tied, rows_g),
        [pltpu.VMEM((256, 256), BF), pltpu.VMEM((256, wide), F32)],
        after=after,
    )


def fold_kernel(which, idx, keep, r1, r2, r3, own, s1, s2, s3):
    me = idx[which]
    for k, ref in enumerate((own, s1, s2, s3)):
        to = lax.rem(me + k, 4)
        ref[...] = keep[to] + r1[to].astype(F32) + r2[to].astype(F32) + r3[to].astype(F32)


def fold(which, idx, keep, recv):
    wide = keep.shape[2]
    return call(
        functools.partial(fold_kernel, which),
        "fold",
        [shape((16, wide), F32)] * 4,
        [SMEM] + [VMEM] * 4,
        (idx, keep, *recv),
    )


def y_shift(v, k):
    return lax.ppermute(v, "par", [(2 * y + c, 2 * ((y + k) % 4) + c) for y in range(4) for c in range(2)])


def core_swap(v):
    return lax.ppermute(v, "par", [(i, i ^ 1) for i in range(8)])


def x_shift(v, k):
    return lax.ppermute(v, "obs", [(4 * z + x, 4 * z + (x + k) % 4) for z in range(4) for x in range(4)])


def z_shift(v, k):
    return lax.ppermute(v, "obs", [(4 * z + x, 4 * ((z + k) % 4) + x) for z in range(4) for x in range(4)])


def exchange(v, axes):
    return lax.all_to_all(v, axes, split_axis=0, concat_axis=0, tiled=True)


def spread(shift, parts):
    got = {k: shift(parts[k - 1], k) for k in (2, 1, 3)}
    return [got[k] for k in (1, 2, 3)]


def local(green, blocks, probes, stations, decay, noise_scale):
    par = lax.axis_index("par")
    obs = lax.axis_index("obs")
    idx = jnp.stack([par % 2, par // 2, obs % 4, obs // 4]).astype(jnp.int32)
    blocks = blocks.T

    mail = info(idx, stations, decay, noise_scale)
    stations_g = exchange(mail, "par")
    mine, send = forward(idx, green, blocks, probes, after=(mail,))
    params = call(params_kernel, "params", shape((16, 8, 128), F32), [VMEM], (stations_g,), after=(send,))

    own, *sends = core_sum(idx, mine, core_swap(send), after=(params,))
    recv = spread(y_shift, sends)
    near, ends, tops, hits = chains(stations_g, green.shape[0], after=(own,))
    coef, station = coefs(exchange(params, "obs"), hits)

    rows_t, pay = group_rows(own, recv, near, ends, coef)
    pieces = [rows_t] + spread(y_shift, [rows_t] * 3)
    pay = exchange(pay, "obs")
    rows_g = end_rows(green, blocks, tops, after=(rows_t,))
    tied = tie(idx, station, pay, after=(rows_g,))
    pieces = pieces + [core_swap(p) for p in pieces]
    product = adjoint(idx, pieces, green, blocks, after=(tied,))
    tied = exchange(tied, "par")
    half0 = finish("x", idx, product, tied, rows_g)
    half1 = finish("z", idx, product, tied, rows_g, after=(half0[1],))

    outs = []
    for (keep, *sends), one, two, which in ((half0, x_shift, z_shift, 3), (half1, z_shift, x_shift, 2)):
        last, *sends = fold(which, idx, keep, spread(one, sends))
        got = spread(two, sends)
        outs.append(last + got[0] + got[1] + got[2])
    return jnp.concatenate(outs, axis=1)


def solution(mesh):
    in_specs = (
        P("obs", "par"),
        P("obs", "par"),
        P("par", None),
        P(("obs", "par")),
        P(("obs", "par")),
        P(("obs", "par")),
    )
    out_specs = P("obs", "par")
    return jax.shard_map(local, mesh=mesh, in_specs=in_specs, out_specs=out_specs, check_vma=False)
```

time: 245 us -> 115 us (0.47)
  waiting for transfers between devices: 132 us -> 6.43 us
  Pallas kernels: 0 us -> 41.4 us
  matrix products: 34.7 us -> 0 us
  starting transfers between devices: 19 us -> 48.2 us
  between operations: 14.6 us -> 1.65 us
  local copies, waits for them, and re-layouts: 17.2 us -> 6.43 us
  other arithmetic: 9.38 us -> 0.77 us
  blocking collectives: 17.9 us -> 9.88 us
    reduce_scatter x2 -> x0, waiting for transfers between devices: 89.5 us -> none  [the longest x1 74.9 us: local(): lax.psum_scatter(adjoint_part, 'obs', scatter_dimension=0, tiled=True)]
    pallas_call x0 -> x14, Pallas kernels: none -> 41.4 us  [call(): pl.pallas_call(body, out_shape=out_shape, in_specs=in_specs + [pl.BlockSp...]
    dot_general x4 -> x0, matrix products: 34.7 us -> none  [the longest x1 16 us: local(): jnp.dot(masked, probes, preferred_element_type=jnp.float32)]
    ppermute x0 -> x23, starting transfers between devices: none -> 29.7 us  [the longest x6 11 us: z_shift(): lax.ppermute(v, 'obs', [(4 * z + x, 4 * ((z + k) % 4) + x) for z in range...]
    all_to_all x2 -> x3, waiting for transfers between devices: 21.3 us -> 0.01 us  [exchange(): return lax.all_to_all(v, axes, split_axis=0, concat_axis=0, tiled=True)]
    all_gather x1 -> x0, waiting for transfers between devices: 21.2 us -> none  [local(): lax.all_gather(own_rows, 'par', axis=0, tiled=True)]
    gather x2 -> x0, local copies, waits for them, and re-layouts: 8.14 us -> none  [the longest x1 4.67 us: local(): whitened[jnp.clip(next_index, 0, slot_total - 1)]]
    all_to_all x1, blocking collectives: 17.9 us -> 9.88 us  [exchange(): return lax.all_to_all(v, axes, split_axis=0, concat_axis=0, tiled=True)]
  transfers between devices with their start and end apart: 5 -> 26, of which waited for: 5 -> 7; matrix products, arithmetic and copies ran while one was open for 2% -> 0% of each run, Pallas kernels for 0% -> 21%
where the time goes in v2:
time: 115 us
  starting transfers between devices  48.2 us (42%)
  Pallas kernels  41.4 us (36%)
  blocking collectives  9.88 us (9%)
  local copies, waits for them, and re-layouts  6.43 us (6%)
  waiting for transfers between devices  6.43 us (6%)
  between operations  1.65 us (1%)
    pallas_call x14, Pallas kernels, call(): pl.pallas_call(body, out_shape=out_shape, in_specs=in_specs + [pl.BlockSp...  41.4 us
    all_to_all x3, starting transfers between devices, exchange(): return lax.all_to_all(v, axes, split_axis=0, concat_axis=0, tiled=True)  18.5 us
    ppermute x6, starting transfers between devices, z_shift(): lax.ppermute(v, 'obs', [(4 * z + x, 4 * ((z + k) % 4) + x) for z in range...  11 us
    ppermute x6, starting transfers between devices, x_shift(): lax.ppermute(v, 'obs', [(4 * z + x, 4 * z + (x + k) % 4) for z in range(4...  10.7 us
    all_to_all x1, blocking collectives, exchange(): return lax.all_to_all(v, axes, split_axis=0, concat_axis=0, tiled=True)  9.88 us
    ppermute x6, starting transfers between devices, y_shift(): lax.ppermute(v, 'par', [(2 * y + c, 2 * ((y + k) % 4) + c) for y in range...  7.72 us
    unnamed x28, local copies, waits for them, and re-layouts  6.43 us
    ppermute x6, waiting for transfers between devices, y_shift(): lax.ppermute(v, 'par', [(2 * y + c, 2 * ((y + k) % 4) + c) for y in range...  3.24 us
  transfers between devices with their start and end apart: 26, of which 7 were waited for; matrix products, arithmetic and copies ran while one was open for 0% of the time, Pallas kernels for 21%

profile of v2, /device:TPU:0, one launch (start us, length us, event | category | flops | bytes accessed | tf_op | source)
XLA Modules:
  0.0 114.8 jit_solution(2142749651581909280)
XLA Ops:
  1.3 0.1 pad_add_fusion.refs_0_
  1.4 0.7 copy-done.5
  2.1 0.6 info.1.refs_4_
  2.6 10.6 %forward.1 = (f32[128,4096]{1,0:T(8,128)S(1)}, f32[128,4096]{1,0:T(8,128)S(1)}) custom-call(s32[4]{0:T(128)S(1)} %pad_add_fusion.refs_0_, bf16[4096,2048]{1,0:T(8,128)(2,1)} %refs_9_.1, s32[16,32]{1,0:T(8,128)} %bitcast.11, bf16[2048,256]{1,0:T(8,128)(2,1)} %refs_3_.1, f32[8,8,128]{2,1,0:T(8,128)S(1)} %info.1.refs_4_), custom_call_target="tpu_custom_call" | custom-call | flops 4294967296 | bytes 16777216 | tf_op jit(solution)/shard_map/forward/pallas_call | solution.py:35
  13.3 0.1 collective-permute-start
  13.4 9.9 %all_to_all.20.refs_0_ = f32[8,8,128]{2,1,0:T(8,128)S(1)} all-to-all(f32[8,8,128]{2,1,0:T(8,128)S(1)} %info.1.refs_4_), channel_id=1, replica_groups=mesh['obs'=16,'par'=8] {'par'}, dimensions={0} | all-to-all | bytes 65536 | tf_op jit(solution)/shard_map/all_to_all | solution.py:488
  23.2 0.6 params.1.refs_3_
  23.9 0.0 collective-permute-done.refs_2_
  23.9 0.7 core_sum.1
  24.6 0.6 collective-permute-start.1
  25.3 2.1 %collective-permute-start.2 = (bf16[32,4096]{1,0:T(8,128)(2,1)S(1)}, bf16[32,4096]{1,0:T(8,128)(2,1)S(1)}, u32[]{:S(2)}, u32[]{:S(2)}) collective-permute-start(bf16[32,4096]{1,0:T(8,128)(2,1)S(1)} %get-tuple-element.39), channel_id=1, source_target_pairs={{0,4},{1,5},{2,6},{3,7},{4,0},{5,1},{6,2},{7,3},{8,12},{9,13},{10,... | collective-permute-start | bytes 786440 | tf_op jit(solution)/shard_map/ppermute | solution.py:472
  27.3 1.1 collective-permute-start.3
  28.4 7.9 %all-to-all-start.1 = ((f32[16,8,128]{2,1,0:T(8,128)}), f32[16,8,128]{2,1,0:T(8,128)S(1)}, u32[]{:S(2)}, u32[]{:S(2)}) async-start(f32[16,8,128]{2,1,0:T(8,128)} %params.1.refs_3_), calls=%async_computation.1 | async-start | bytes 131072 | tf_op jit(solution)/shard_map/all_to_all | solution.py:488
  36.3 3.6 %chains.1 = (bf16[16,256,256]{2,1,0:T(8,128)(2,1)S(1)}, bf16[256,4096]{1,0:T(8,128)(2,1)S(1)}, bf16[256,4096]{1,0:T(8,128)(2,1)S(1)}, bf16[128,4096]{1,0:T(8,128)(2,1)S(1)}) custom-call(f32[8,8,128]{2,1,0:T(8,128)S(1)} %all_to_all.20.refs_0_, f32[32,4096]{1,0:T(8,128)S(1)} %get-tuple-element.37.refs_1_.refs_0_), custom_call_target="tpu_custom_call" | custom-call | bytes 12582912 | tf_op jit(solution)/shard_map/chains/pallas_call | solution.py:35
  40.0 1.3 %copy-done = bf16[256,4096]{1,0:T(8,128)(2,1)} copy-done((bf16[256,4096]{1,0:T(8,128)(2,1)}, bf16[256,4096]{1,0:T(8,128)(2,1)S(1)}, u32[]{:S(2)}) %copy-start) | copy-done | bytes 2097176
  41.3 1.3 %copy-done.1 = bf16[16,256,256]{2,1,0:T(8,128)(2,1)} copy-done((bf16[16,256,256]{2,1,0:T(8,128)(2,1)}, bf16[16,256,256]{2,1,0:T(8,128)(2,1)S(1)}, u32[]{:S(2)}) %copy-start.1) | copy-done | bytes 2097176
  42.7 1.4 %copy-done.2 = bf16[256,4096]{1,0:T(8,128)(2,1)} copy-done((bf16[256,4096]{1,0:T(8,128)(2,1)}, bf16[256,4096]{1,0:T(8,128)(2,1)S(1)}, u32[]{:S(2)}) %copy-start.2) | copy-done | bytes 2097176
  44.0 0.3 coefs.1
  44.3 0.0 collective-permute-done.1.refs_1_
  44.3 0.0 collective-permute-done.2.refs_2_
  44.4 0.6 copy-done.11
  45.0 0.2 copy-done.12
  45.2 0.1 copy-done.13
  45.3 3.7 %group_rows.1 = (bf16[32,4096]{1,0:T(8,128)(2,1)S(1)}, bf16[16,96,128]{2,1,0:T(8,128)(2,1)}) custom-call(f32[32,4096]{1,0:T(8,128)} %copy-done.3, bf16[32,4096]{1,0:T(8,128)(2,1)} %copy-done.11, bf16[32,4096]{1,0:T(8,128)(2,1)} %copy-done.12, bf16[32,4096]{1,0:T(8,128)(2,1)} %copy-done.13, bf16[16,256,256]{2,1,0:T(8,128)(2,1)} %copy-done.1, ...), custom_call_target="tpu_custom_call" | custom-call | tf_op jit(solution)/shard_map/group_rows/pallas_call | solution.py:35
  49.0 1.0 collective-permute-start.6
  50.0 2.1 %collective-permute-start.5 = (bf16[32,4096]{1,0:T(8,128)(2,1)S(1)}, bf16[32,4096]{1,0:T(8,128)(2,1)S(1)}, u32[]{:S(2)}, u32[]{:S(2)}) collective-permute-start(bf16[32,4096]{1,0:T(8,128)(2,1)S(1)} %get-tuple-element.45.refs_3_.refs_1_), channel_id=1, source_target_pairs={{0,4},{1,5},{2,6},{3,7},{4,0},{5,1},{6,2},{7,3},{8,12},{9,13},{10,... | collective-permute-start | bytes 786440 | tf_op jit(solution)/shard_map/ppermute | solution.py:472
  52.1 0.9 collective-permute-start.4
  53.0 7.2 %all-to-all-start.2 = ((bf16[16,96,128]{2,1,0:T(8,128)(2,1)}), bf16[16,96,128]{2,1,0:T(8,128)(2,1)S(1)}, u32[]{:S(2)}, u32[]{:S(2)}) async-start(bf16[16,96,128]{2,1,0:T(8,128)(2,1)} %get-tuple-element.47), calls=%async_computation.2 | async-start | bytes 786432 | tf_op jit(solution)/shard_map/all_to_all | solution.py:488
  60.2 0.3 collective-permute-start.10
  60.5 0.3 collective-permute-done.5.refs_3_
  60.8 0.0 collective-permute-start.9
  60.8 2.9 %collective-permute-done.4.refs_2_ = bf16[32,4096]{1,0:T(8,128)(2,1)S(1)} collective-permute-done((bf16[32,4096]{1,0:T(8,128)(2,1)S(1)}, bf16[32,4096]{1,0:T(8,128)(2,1)S(1)}, u32[]{:S(2)}, u32[]{:S(2)}) %collective-permute-start.4) | collective-permute-done | bytes 262176 | tf_op jit(solution)/shard_map/ppermute | solution.py:472
  63.7 0.0 collective-permute-start.8
  63.7 8.3 %end_rows.1.refs_3_ = bf16[256,2048]{1,0:T(8,128)(2,1)S(1)} custom-call(bf16[4096,2048]{1,0:T(8,128)(2,1)} %refs_9_.1, s32[16,32]{1,0:T(8,128)} %bitcast.12, bf16[256,4096]{1,0:T(8,128)(2,1)} %copy-done, bf16[32,4096]{1,0:T(8,128)(2,1)S(1)} %get-tuple-element.45.refs_3_.refs_1_), custom_call_target="tpu_custom_call" | custom-call | flops 4294967296 | bytes 16777216 | tf_op jit(solution)/shard_map/end_rows/pallas_call | solution.py:35
  72.1 0.0 all-to-all-done.2.refs_2_
  72.1 1.3 %tie.1.refs_11_ = bf16[8,32,256]{2,1,0:T(8,128)(2,1)} custom-call(s32[4]{0:T(128)S(1)} %pad_add_fusion.refs_0_, f32[8,128]{1,0:T(8,128)S(1)} %get-tuple-element.46.refs_1_, bf16[16,96,128]{2,1,0:T(8,128)(2,1)S(1)} %all-to-all-done.2.refs_2_, bf16[256,2048]{1,0:T(8,128)(2,1)S(1)} %end_rows.1.refs_3_), custom_call_target="tpu_custom_call" | custom-call | tf_op jit(solution)/shard_map/tie/pallas_call | solution.py:35
  73.4 3.4 %all-to-all-start.3 = ((bf16[8,32,256]{2,1,0:T(8,128)(2,1)}), bf16[8,32,256]{2,1,0:T(8,128)(2,1)S(1)}, u32[]{:S(2)}, u32[]{:S(2)}) async-start(bf16[8,32,256]{2,1,0:T(8,128)(2,1)} %tie.1.refs_11_), calls=%async_computation.3 | async-start | bytes 262144 | tf_op jit(solution)/shard_map/all_to_all | solution.py:488
  76.7 0.0 collective-permute-done.7.refs_5_
  76.8 0.0 collective-permute-done.10.refs_8_
  76.8 0.7 copy-done.9
  77.5 0.1 copy-done.10
  77.6 8.6 %adjoint.1.refs_1_ = f32[256,2048]{1,0:T(8,128)S(1)} custom-call(s32[4]{0:T(128)S(1)} %pad_add_fusion.refs_0_, bf16[32,4096]{1,0:T(8,128)(2,1)} %copy-done.4, bf16[32,4096]{1,0:T(8,128)(2,1)} %copy-done.8, bf16[32,4096]{1,0:T(8,128)(2,1)} %copy-done.7, bf16[32,4096]{1,0:T(8,128)(2,1)} %copy-done.6, bf16[32,4096]{1,0:T(8,128)(2,1)} %copy-done.9, ...), custom_call_target="tpu_custom_call" | custom-call | flops 4294967296 | bytes 16777216 | tf_op jit(solution)/shard_map/adjoint/pallas_call | solution.py:35
  86.2 0.9 finish_x.1
  87.1 0.9 finish_z.1
  88.1 1.7 %collective-permute-start.17 = (bf16[4,16,1024]{2,1,0:T(8,128)(2,1)S(1)}, bf16[4,16,1024]{2,1,0:T(8,128)(2,1)S(1)}, u32[]{:S(2)}, u32[]{:S(2)}) collective-permute-start(bf16[4,16,1024]{2,1,0:T(8,128)(2,1)S(1)} %get-tuple-element.58), channel_id=1, source_target_pairs={{0,32},{8,40},{16,48},{24,56},{32,64},{40,72},{48,80},{56,88},{64,... | collective-permute-start | bytes 393224 | tf_op jit(solution)/shard_map/ppermute | solution.py:484
  89.8 2.7 %collective-permute-start.18 = (bf16[4,16,1024]{2,1,0:T(8,128)(2,1)S(1)}, bf16[4,16,1024]{2,1,0:T(8,128)(2,1)S(1)}, u32[]{:S(2)}, u32[]{:S(2)}) collective-permute-start(bf16[4,16,1024]{2,1,0:T(8,128)(2,1)S(1)} %get-tuple-element.59), channel_id=1, source_target_pairs={{0,64},{8,72},{16,80},{24,88},{32,96},{40,104},{48,112},{56,120},{... | collective-permute-start | bytes 393224 | tf_op jit(solution)/shard_map/ppermute | solution.py:484
  92.5 1.4 %collective-permute-start.19 = (bf16[4,16,1024]{2,1,0:T(8,128)(2,1)S(1)}, bf16[4,16,1024]{2,1,0:T(8,128)(2,1)S(1)}, u32[]{:S(2)}, u32[]{:S(2)}) collective-permute-start(bf16[4,16,1024]{2,1,0:T(8,128)(2,1)S(1)} %get-tuple-element.60), channel_id=1, source_target_pairs={{0,96},{8,104},{16,112},{24,120},{32,0},{40,8},{48,16},{56,24},{64... | collective-permute-start | bytes 393224 | tf_op jit(solution)/shard_map/ppermute | solution.py:484
  93.9 3.0 %collective-permute-start.12 = (bf16[4,16,1024]{2,1,0:T(8,128)(2,1)S(1)}, bf16[4,16,1024]{2,1,0:T(8,128)(2,1)S(1)}, u32[]{:S(2)}, u32[]{:S(2)}) collective-permute-start(bf16[4,16,1024]{2,1,0:T(8,128)(2,1)S(1)} %get-tuple-element.51), channel_id=1, source_target_pairs={{0,16},{8,24},{16,0},{24,8},{32,48},{40,56},{48,32},{56,40},{64,80... | collective-permute-start | bytes 393224 | tf_op jit(solution)/shard_map/ppermute | solution.py:480
  96.9 1.2 %collective-permute-start.13 = (bf16[4,16,1024]{2,1,0:T(8,128)(2,1)S(1)}, bf16[4,16,1024]{2,1,0:T(8,128)(2,1)S(1)}, u32[]{:S(2)}, u32[]{:S(2)}) collective-permute-start(bf16[4,16,1024]{2,1,0:T(8,128)(2,1)S(1)} %get-tuple-element.52), channel_id=1, source_target_pairs={{0,24},{8,0},{16,8},{24,16},{32,56},{40,32},{48,40},{56,48},{64,88... | collective-permute-start | bytes 393224 | tf_op jit(solution)/shard_map/ppermute | solution.py:480
  98.0 0.9 collective-permute-start.11
  98.9 0.1 collective-permute-done.18.refs_3_
  99.0 0.6 fold.3
  99.6 1.5 %collective-permute-start.20 = (f32[16,1024]{1,0:T(8,128)S(1)}, f32[16,1024]{1,0:T(8,128)S(1)}, u32[]{:S(2)}, u32[]{:S(2)}) collective-permute-start(f32[16,1024]{1,0:T(8,128)S(1)} %get-tuple-element.62), channel_id=1, source_target_pairs={{0,8},{8,16},{16,24},{24,0},{32,40},{40,48},{48,56},{56,32},{64,72... | collective-permute-start | bytes 196616 | tf_op jit(solution)/shard_map/ppermute | solution.py:480
  101.2 2.7 %collective-permute-start.21 = (f32[16,1024]{1,0:T(8,128)S(1)}, f32[16,1024]{1,0:T(8,128)S(1)}, u32[]{:S(2)}, u32[]{:S(2)}) collective-permute-start(f32[16,1024]{1,0:T(8,128)S(1)} %get-tuple-element.63), channel_id=1, source_target_pairs={{0,16},{8,24},{16,0},{24,8},{32,48},{40,56},{48,32},{56,40},{64,80... | collective-permute-start | bytes 196616 | tf_op jit(solution)/shard_map/ppermute | solution.py:480
  103.8 1.5 %collective-permute-start.22 = (f32[16,1024]{1,0:T(8,128)S(1)}, f32[16,1024]{1,0:T(8,128)S(1)}, u32[]{:S(2)}, u32[]{:S(2)}) collective-permute-start(f32[16,1024]{1,0:T(8,128)S(1)} %get-tuple-element.64), channel_id=1, source_target_pairs={{0,24},{8,0},{16,8},{24,16},{32,56},{40,32},{48,40},{56,48},{64,88... | collective-permute-start | bytes 196616 | tf_op jit(solution)/shard_map/ppermute | solution.py:480
  105.3 0.3 collective-permute-done.11.refs_2_
  105.6 0.6 fold.2
  106.2 1.2 %collective-permute-start.14 = (f32[16,1024]{1,0:T(8,128)S(1)}, f32[16,1024]{1,0:T(8,128)S(1)}, u32[]{:S(2)}, u32[]{:S(2)}) collective-permute-start(f32[16,1024]{1,0:T(8,128)S(1)} %get-tuple-element.54), channel_id=1, source_target_pairs={{0,32},{8,40},{16,48},{24,56},{32,64},{40,72},{48,80},{56,88},{64,... | collective-permute-start | bytes 196616 | tf_op jit(solution)/shard_map/ppermute | solution.py:484
  107.4 2.4 %collective-permute-start.15 = (f32[16,1024]{1,0:T(8,128)S(1)}, f32[16,1024]{1,0:T(8,128)S(1)}, u32[]{:S(2)}, u32[]{:S(2)}) collective-permute-start(f32[16,1024]{1,0:T(8,128)S(1)} %get-tuple-element.55), channel_id=1, source_target_pairs={{0,64},{8,72},{16,80},{24,88},{32,96},{40,104},{48,112},{56,120},{... | collective-permute-start | bytes 196616 | tf_op jit(solution)/shard_map/ppermute | solution.py:484
  109.8 1.5 %collective-permute-start.16 = (f32[16,1024]{1,0:T(8,128)S(1)}, f32[16,1024]{1,0:T(8,128)S(1)}, u32[]{:S(2)}, u32[]{:S(2)}) collective-permute-start(f32[16,1024]{1,0:T(8,128)S(1)} %get-tuple-element.56), channel_id=1, source_target_pairs={{0,96},{8,104},{16,112},{24,120},{32,0},{40,8},{48,16},{56,24},{64... | collective-permute-start | bytes 196616 | tf_op jit(solution)/shard_map/ppermute | solution.py:484
  111.4 0.4 collective-permute-done.14
  111.8 1.4 %collective-permute-done.15 = f32[16,1024]{1,0:T(8,128)S(1)} collective-permute-done((f32[16,1024]{1,0:T(8,128)S(1)}, f32[16,1024]{1,0:T(8,128)S(1)}, u32[]{:S(2)}, u32[]{:S(2)}) %collective-permute-start.15) | collective-permute-done | bytes 65568 | tf_op jit(solution)/shard_map/ppermute | solution.py:484
  113.2 0.9 collective-permute-done.16
  114.1 0.7 pad_maximum_fusion
  (35 shorter events, 0.1 us)
Async XLA Ops:
  1.4 0.7 copy-start.5
  13.3 10.6 %collective-permute-start = (f32[128,4096]{1,0:T(8,128)S(1)}, f32[128,4096]{1,0:T(8,128)S(1)}, u32[]{:S(2)}, u32[]{:S(2)}) collective-permute-start(f32[128,4096]{1,0:T(8,128)S(1)} %get-tuple-element.36.refs_1_), channel_id=1, source_target_pairs={{0,1},{1,0},{2,3},{3,2},{4,5},{5,4},{6,7},{7,6},{8,9},{9,8},{10,11... | collective-permute-start | bytes 6291464 | tf_op jit(solution)/shard_map/ppermute | solution.py:476
  24.6 19.7 %copy-start.3 = (f32[32,4096]{1,0:T(8,128)}, f32[32,4096]{1,0:T(8,128)S(1)}, u32[]{:S(2)}) copy-start(f32[32,4096]{1,0:T(8,128)S(1)} %get-tuple-element.37.refs_1_.refs_0_) | copy-start | bytes 1572868
  24.6 19.7 %collective-permute-start.1 = (bf16[32,4096]{1,0:T(8,128)(2,1)S(1)}, bf16[32,4096]{1,0:T(8,128)(2,1)S(1)}, u32[]{:S(2)}, u32[]{:S(2)}) collective-permute-start(bf16[32,4096]{1,0:T(8,128)(2,1)S(1)} %get-tuple-element.38), channel_id=1, source_target_pairs={{0,2},{1,3},{2,4},{3,5},{4,6},{5,7},{6,0},{7,1},{8,10},{9,11},{10,... | collective-permute-start | bytes 786440 | tf_op jit(solution)/shard_map/ppermute | solution.py:472
  25.3 19.1 %collective-permute-start.2 = (bf16[32,4096]{1,0:T(8,128)(2,1)S(1)}, bf16[32,4096]{1,0:T(8,128)(2,1)S(1)}, u32[]{:S(2)}, u32[]{:S(2)}) collective-permute-start(bf16[32,4096]{1,0:T(8,128)(2,1)S(1)} %get-tuple-element.39), channel_id=1, source_target_pairs={{0,4},{1,5},{2,6},{3,7},{4,0},{5,1},{6,2},{7,3},{8,12},{9,13},{10,... | collective-permute-start | bytes 786440 | tf_op jit(solution)/shard_map/ppermute | solution.py:472
  27.3 17.0 %collective-permute-start.3 = (bf16[32,4096]{1,0:T(8,128)(2,1)S(1)}, bf16[32,4096]{1,0:T(8,128)(2,1)S(1)}, u32[]{:S(2)}, u32[]{:S(2)}) collective-permute-start(bf16[32,4096]{1,0:T(8,128)(2,1)S(1)} %get-tuple-element.40), channel_id=1, source_target_pairs={{0,6},{1,7},{2,0},{3,1},{4,2},{5,3},{6,4},{7,5},{8,14},{9,15},{10,... | collective-permute-start | bytes 786440 | tf_op jit(solution)/shard_map/ppermute | solution.py:472
  28.4 15.6 %all-to-all-start.1 = ((f32[16,8,128]{2,1,0:T(8,128)}), f32[16,8,128]{2,1,0:T(8,128)S(1)}, u32[]{:S(2)}, u32[]{:S(2)}) async-start(f32[16,8,128]{2,1,0:T(8,128)} %params.1.refs_3_), calls=%async_computation.1 | async-start | bytes 131072 | tf_op jit(solution)/shard_map/all_to_all | solution.py:488
  40.0 1.3 %copy-start = (bf16[256,4096]{1,0:T(8,128)(2,1)}, bf16[256,4096]{1,0:T(8,128)(2,1)S(1)}, u32[]{:S(2)}) copy-start(bf16[256,4096]{1,0:T(8,128)(2,1)S(1)} %get-tuple-element.48.refs_2_) | copy-start | bytes 6291460
  41.3 1.3 %copy-start.1 = (bf16[16,256,256]{2,1,0:T(8,128)(2,1)}, bf16[16,256,256]{2,1,0:T(8,128)(2,1)S(1)}, u32[]{:S(2)}) copy-start(bf16[16,256,256]{2,1,0:T(8,128)(2,1)S(1)} %get-tuple-element.41.refs_4_) | copy-start | bytes 6291460
  42.7 1.4 %copy-start.2 = (bf16[256,4096]{1,0:T(8,128)(2,1)}, bf16[256,4096]{1,0:T(8,128)(2,1)S(1)}, u32[]{:S(2)}) copy-start(bf16[256,4096]{1,0:T(8,128)(2,1)S(1)} %get-tuple-element.42.refs_5_) | copy-start | bytes 6291460
  44.3 0.7 copy-start.11
  44.3 0.8 copy-start.12
  44.4 0.9 copy-start.13
  49.0 23.0 %copy-start.4 = (bf16[32,4096]{1,0:T(8,128)(2,1)}, bf16[32,4096]{1,0:T(8,128)(2,1)S(1)}, u32[]{:S(2)}) copy-start(bf16[32,4096]{1,0:T(8,128)(2,1)S(1)} %get-tuple-element.45.refs_3_.refs_1_) | copy-start | bytes 786436
  49.0 11.2 %collective-permute-start.6 = (bf16[32,4096]{1,0:T(8,128)(2,1)S(1)}, bf16[32,4096]{1,0:T(8,128)(2,1)S(1)}, u32[]{:S(2)}, u32[]{:S(2)}) collective-permute-start(bf16[32,4096]{1,0:T(8,128)(2,1)S(1)} %get-tuple-element.45.refs_3_.refs_1_), channel_id=1, source_target_pairs={{0,6},{1,7},{2,0},{3,1},{4,2},{5,3},{6,4},{7,5},{8,14},{9,15},{10,... | collective-permute-start | bytes 786440 | tf_op jit(solution)/shard_map/ppermute | solution.py:472
  50.0 10.7 %collective-permute-start.5 = (bf16[32,4096]{1,0:T(8,128)(2,1)S(1)}, bf16[32,4096]{1,0:T(8,128)(2,1)S(1)}, u32[]{:S(2)}, u32[]{:S(2)}) collective-permute-start(bf16[32,4096]{1,0:T(8,128)(2,1)S(1)} %get-tuple-element.45.refs_3_.refs_1_), channel_id=1, source_target_pairs={{0,4},{1,5},{2,6},{3,7},{4,0},{5,1},{6,2},{7,3},{8,12},{9,13},{10,... | collective-permute-start | bytes 786440 | tf_op jit(solution)/shard_map/ppermute | solution.py:472
  52.1 11.7 %collective-permute-start.4 = (bf16[32,4096]{1,0:T(8,128)(2,1)S(1)}, bf16[32,4096]{1,0:T(8,128)(2,1)S(1)}, u32[]{:S(2)}, u32[]{:S(2)}) collective-permute-start(bf16[32,4096]{1,0:T(8,128)(2,1)S(1)} %get-tuple-element.45.refs_3_.refs_1_), channel_id=1, source_target_pairs={{0,2},{1,3},{2,4},{3,5},{4,6},{5,7},{6,0},{7,1},{8,10},{9,11},{10,... | collective-permute-start | bytes 786440 | tf_op jit(solution)/shard_map/ppermute | solution.py:472
  53.0 23.8 %collective-permute-start.7 = (bf16[32,4096]{1,0:T(8,128)(2,1)S(1)}, bf16[32,4096]{1,0:T(8,128)(2,1)S(1)}, u32[]{:S(2)}, u32[]{:S(2)}) collective-permute-start(bf16[32,4096]{1,0:T(8,128)(2,1)S(1)} %get-tuple-element.45.refs_3_.refs_1_), channel_id=1, source_target_pairs={{0,1},{1,0},{2,3},{3,2},{4,5},{5,4},{6,7},{7,6},{8,9},{9,8},{10,11... | collective-permute-start | bytes 786440 | tf_op jit(solution)/shard_map/ppermute | solution.py:476
  53.0 19.1 %all-to-all-start.2 = ((bf16[16,96,128]{2,1,0:T(8,128)(2,1)}), bf16[16,96,128]{2,1,0:T(8,128)(2,1)S(1)}, u32[]{:S(2)}, u32[]{:S(2)}) async-start(bf16[16,96,128]{2,1,0:T(8,128)(2,1)} %get-tuple-element.47), calls=%async_computation.2 | async-start | bytes 786432 | tf_op jit(solution)/shard_map/all_to_all | solution.py:488
  60.2 11.9 %copy-start.6 = (bf16[32,4096]{1,0:T(8,128)(2,1)}, bf16[32,4096]{1,0:T(8,128)(2,1)S(1)}, u32[]{:S(2)}) copy-start(bf16[32,4096]{1,0:T(8,128)(2,1)S(1)} %collective-permute-done.6.refs_4_) | copy-start | bytes 786436
  60.2 16.6 %collective-permute-start.10 = (bf16[32,4096]{1,0:T(8,128)(2,1)S(1)}, bf16[32,4096]{1,0:T(8,128)(2,1)S(1)}, u32[]{:S(2)}, u32[]{:S(2)}) collective-permute-start(bf16[32,4096]{1,0:T(8,128)(2,1)S(1)} %collective-permute-done.6.refs_4_), channel_id=1, source_target_pairs={{0,1},{1,0},{2,3},{3,2},{4,5},{5,4},{6,7},{7,6},{8,9},{9,8},{10,11... | collective-permute-start | bytes 786440 | tf_op jit(solution)/shard_map/ppermute | solution.py:476
  60.8 11.3 %copy-start.7 = (bf16[32,4096]{1,0:T(8,128)(2,1)}, bf16[32,4096]{1,0:T(8,128)(2,1)S(1)}, u32[]{:S(2)}) copy-start(bf16[32,4096]{1,0:T(8,128)(2,1)S(1)} %collective-permute-done.5.refs_3_) | copy-start | bytes 786436
  60.8 16.0 %collective-permute-start.9 = (bf16[32,4096]{1,0:T(8,128)(2,1)S(1)}, bf16[32,4096]{1,0:T(8,128)(2,1)}, u32[]{:S(2)}, u32[]{:S(2)}) collective-permute-start(bf16[32,4096]{1,0:T(8,128)(2,1)S(1)} %collective-permute-done.5.refs_3_), channel_id=1, source_target_pairs={{0,1},{1,0},{2,3},{3,2},{4,5},{5,4},{6,7},{7,6},{8,9},{9,8},{10,11... | collective-permute-start | bytes 786440 | tf_op jit(solution)/shard_map/ppermute | solution.py:476
  63.7 8.3 %copy-start.8 = (bf16[32,4096]{1,0:T(8,128)(2,1)}, bf16[32,4096]{1,0:T(8,128)(2,1)S(1)}, u32[]{:S(2)}) copy-start(bf16[32,4096]{1,0:T(8,128)(2,1)S(1)} %collective-permute-done.4.refs_2_) | copy-start | bytes 786436
  63.7 13.8 %collective-permute-start.8 = (bf16[32,4096]{1,0:T(8,128)(2,1)S(1)}, bf16[32,4096]{1,0:T(8,128)(2,1)}, u32[]{:S(2)}, u32[]{:S(2)}) collective-permute-start(bf16[32,4096]{1,0:T(8,128)(2,1)S(1)} %collective-permute-done.4.refs_2_), channel_id=1, source_target_pairs={{0,1},{1,0},{2,3},{3,2},{4,5},{5,4},{6,7},{7,6},{8,9},{9,8},{10,11... | collective-permute-start | bytes 786440 | tf_op jit(solution)/shard_map/ppermute | solution.py:476
  73.4 12.8 %all-to-all-start.3 = ((bf16[8,32,256]{2,1,0:T(8,128)(2,1)}), bf16[8,32,256]{2,1,0:T(8,128)(2,1)S(1)}, u32[]{:S(2)}, u32[]{:S(2)}) async-start(bf16[8,32,256]{2,1,0:T(8,128)(2,1)} %tie.1.refs_11_), calls=%async_computation.3 | async-start | bytes 262144 | tf_op jit(solution)/shard_map/all_to_all | solution.py:488
  76.8 0.7 copy-start.9
  76.8 0.8 copy-start.10
  88.1 10.0 %collective-permute-start.17 = (bf16[4,16,1024]{2,1,0:T(8,128)(2,1)S(1)}, bf16[4,16,1024]{2,1,0:T(8,128)(2,1)S(1)}, u32[]{:S(2)}, u32[]{:S(2)}) collective-permute-start(bf16[4,16,1024]{2,1,0:T(8,128)(2,1)S(1)} %get-tuple-element.58), channel_id=1, source_target_pairs={{0,32},{8,40},{16,48},{24,56},{32,64},{40,72},{48,80},{56,88},{64,... | collective-permute-start | bytes 393224 | tf_op jit(solution)/shard_map/ppermute | solution.py:484
  89.8 9.2 %collective-permute-start.18 = (bf16[4,16,1024]{2,1,0:T(8,128)(2,1)S(1)}, bf16[4,16,1024]{2,1,0:T(8,128)(2,1)S(1)}, u32[]{:S(2)}, u32[]{:S(2)}) collective-permute-start(bf16[4,16,1024]{2,1,0:T(8,128)(2,1)S(1)} %get-tuple-element.59), channel_id=1, source_target_pairs={{0,64},{8,72},{16,80},{24,88},{32,96},{40,104},{48,112},{56,120},{... | collective-permute-start | bytes 393224 | tf_op jit(solution)/shard_map/ppermute | solution.py:484
  92.5 6.5 %collective-permute-start.19 = (bf16[4,16,1024]{2,1,0:T(8,128)(2,1)S(1)}, bf16[4,16,1024]{2,1,0:T(8,128)(2,1)S(1)}, u32[]{:S(2)}, u32[]{:S(2)}) collective-permute-start(bf16[4,16,1024]{2,1,0:T(8,128)(2,1)S(1)} %get-tuple-element.60), channel_id=1, source_target_pairs={{0,96},{8,104},{16,112},{24,120},{32,0},{40,8},{48,16},{56,24},{64... | collective-permute-start | bytes 393224 | tf_op jit(solution)/shard_map/ppermute | solution.py:484
  93.9 9.9 %collective-permute-start.12 = (bf16[4,16,1024]{2,1,0:T(8,128)(2,1)S(1)}, bf16[4,16,1024]{2,1,0:T(8,128)(2,1)S(1)}, u32[]{:S(2)}, u32[]{:S(2)}) collective-permute-start(bf16[4,16,1024]{2,1,0:T(8,128)(2,1)S(1)} %get-tuple-element.51), channel_id=1, source_target_pairs={{0,16},{8,24},{16,0},{24,8},{32,48},{40,56},{48,32},{56,40},{64,80... | collective-permute-start | bytes 393224 | tf_op jit(solution)/shard_map/ppermute | solution.py:480
  96.9 8.4 %collective-permute-start.13 = (bf16[4,16,1024]{2,1,0:T(8,128)(2,1)S(1)}, bf16[4,16,1024]{2,1,0:T(8,128)(2,1)S(1)}, u32[]{:S(2)}, u32[]{:S(2)}) collective-permute-start(bf16[4,16,1024]{2,1,0:T(8,128)(2,1)S(1)} %get-tuple-element.52), channel_id=1, source_target_pairs={{0,24},{8,0},{16,8},{24,16},{32,56},{40,32},{48,40},{56,48},{64,88... | collective-permute-start | bytes 393224 | tf_op jit(solution)/shard_map/ppermute | solution.py:480
  98.0 7.6 %collective-permute-start.11 = (bf16[4,16,1024]{2,1,0:T(8,128)(2,1)S(1)}, bf16[4,16,1024]{2,1,0:T(8,128)(2,1)S(1)}, u32[]{:S(2)}, u32[]{:S(2)}) collective-permute-start(bf16[4,16,1024]{2,1,0:T(8,128)(2,1)S(1)} %get-tuple-element.50.refs_4_), channel_id=1, source_target_pairs={{0,8},{8,16},{16,24},{24,0},{32,40},{40,48},{48,56},{56,32},{64,72... | collective-permute-start | bytes 393224 | tf_op jit(solution)/shard_map/ppermute | solution.py:480
  99.6 10.2 %collective-permute-start.20 = (f32[16,1024]{1,0:T(8,128)S(1)}, f32[16,1024]{1,0:T(8,128)S(1)}, u32[]{:S(2)}, u32[]{:S(2)}) collective-permute-start(f32[16,1024]{1,0:T(8,128)S(1)} %get-tuple-element.62), channel_id=1, source_target_pairs={{0,8},{8,16},{16,24},{24,0},{32,40},{40,48},{48,56},{56,32},{64,72... | collective-permute-start | bytes 196616 | tf_op jit(solution)/shard_map/ppermute | solution.py:480
  101.2 10.2 %collective-permute-start.21 = (f32[16,1024]{1,0:T(8,128)S(1)}, f32[16,1024]{1,0:T(8,128)S(1)}, u32[]{:S(2)}, u32[]{:S(2)}) collective-permute-start(f32[16,1024]{1,0:T(8,128)S(1)} %get-tuple-element.63), channel_id=1, source_target_pairs={{0,16},{8,24},{16,0},{24,8},{32,48},{40,56},{48,32},{56,40},{64,80... | collective-permute-start | bytes 196616 | tf_op jit(solution)/shard_map/ppermute | solution.py:480
  103.8 7.5 %collective-permute-start.22 = (f32[16,1024]{1,0:T(8,128)S(1)}, f32[16,1024]{1,0:T(8,128)S(1)}, u32[]{:S(2)}, u32[]{:S(2)}) collective-permute-start(f32[16,1024]{1,0:T(8,128)S(1)} %get-tuple-element.64), channel_id=1, source_target_pairs={{0,24},{8,0},{16,8},{24,16},{32,56},{40,32},{48,40},{56,48},{64,88... | collective-permute-start | bytes 196616 | tf_op jit(solution)/shard_map/ppermute | solution.py:480
  106.2 5.5 %collective-permute-start.14 = (f32[16,1024]{1,0:T(8,128)S(1)}, f32[16,1024]{1,0:T(8,128)S(1)}, u32[]{:S(2)}, u32[]{:S(2)}) collective-permute-start(f32[16,1024]{1,0:T(8,128)S(1)} %get-tuple-element.54), channel_id=1, source_target_pairs={{0,32},{8,40},{16,48},{24,56},{32,64},{40,72},{48,80},{56,88},{64,... | collective-permute-start | bytes 196616 | tf_op jit(solution)/shard_map/ppermute | solution.py:484
  107.4 5.8 %collective-permute-start.15 = (f32[16,1024]{1,0:T(8,128)S(1)}, f32[16,1024]{1,0:T(8,128)S(1)}, u32[]{:S(2)}, u32[]{:S(2)}) collective-permute-start(f32[16,1024]{1,0:T(8,128)S(1)} %get-tuple-element.55), channel_id=1, source_target_pairs={{0,64},{8,72},{16,80},{24,88},{32,96},{40,104},{48,112},{56,120},{... | collective-permute-start | bytes 196616 | tf_op jit(solution)/shard_map/ppermute | solution.py:484
  109.8 4.3 %collective-permute-start.16 = (f32[16,1024]{1,0:T(8,128)S(1)}, f32[16,1024]{1,0:T(8,128)S(1)}, u32[]{:S(2)}, u32[]{:S(2)}) collective-permute-start(f32[16,1024]{1,0:T(8,128)S(1)} %get-tuple-element.56), channel_id=1, source_target_pairs={{0,96},{8,104},{16,112},{24,120},{32,0},{40,8},{48,16},{56,24},{64... | collective-permute-start | bytes 196616 | tf_op jit(solution)/shard_map/ppermute | solution.py:484

commit v3 on v2

--- a/solution.py
+++ b/solution.py
@@ -25,7 +25,7 @@
     return jax.ShapeDtypeStruct(dims, dtype)
 
 
-def call(kernel, name, out_shape, in_specs, args, scratch=(), mib=16, flops=0, data=0, after=()):
+def call(kernel, name, out_shape, in_specs, args, scratch=(), mib=16, flops=0, data=0, after=(), out_specs=None):
     single = not isinstance(out_shape, list)
     n, m = len(args), len(after)
 
@@ -36,7 +36,7 @@
         body,
         out_shape=out_shape,
         in_specs=in_specs + [pl.BlockSpec(memory_space=pl.ANY)] * m,
-        out_specs=VMEM if single else [VMEM] * len(out_shape),
+        out_specs=out_specs or (VMEM if single else [VMEM] * len(out_shape)),
         scratch_shapes=list(scratch),
         compiler_params=pltpu.CompilerParams(vmem_limit_bytes=mib * MB),
         cost_estimate=pl.CostEstimate(flops=flops, bytes_accessed=data, transcendentals=0),
@@ -80,7 +80,7 @@
     ]
     for copy in small:
         copy.start()
-    for i in range(3):
+    for i in range(2):
         fetch(green, 0, buf, sem, i).start()
     small[0].wait()
     expand(own_blocks, gate)
@@ -90,8 +90,8 @@
         panel[pl.ds(at, 128), :] = own_probes[:, part * 128 : (part + 1) * 128].T
     for i in range(steps):
         fetch(green, 0, buf, sem, i).wait()
-        if i + 3 < steps:
-            fetch(green, 0, buf, sem, i + 3).start()
+        if i + 2 < steps:
+            fetch(green, 0, buf, sem, i + 2).start()
         mask_rows(buf, gate, i, tile, 0)
         at = slice(i * tile, (i + 1) * tile)
         part = lax.dot_general(panel[...], buf[at, :], NT, preferred_element_type=F32)
@@ -168,12 +168,19 @@
     sums[...] = jnp.broadcast_to(jnp.sum(table[...], axis=0)[None], sums.shape)
 
 
-def chain_kernel(table, near, ends, tops, hits):
+def chain_kernel(table, near_h, ends_h, tops_h, hits, near, ends, tops, sem):
     held = []
+    copies = []
+
+    def send(src, dst, i):
+        copies.append(pltpu.make_async_copy(src, dst, sem.at[i]))
+        copies[-1].start()
+
     here = lax.broadcasted_iota(jnp.int32, (CH, CH), 0)
     there = lax.broadcasted_iota(jnp.int32, (CH, CH), 1)
     sid = lax.broadcasted_iota(jnp.int32, (128, CH), 0).astype(F32)
-    for b in range(hits.shape[1] // CH):
+    n = hits.shape[1] // CH
+    for b in range(n):
         at = slice(b * CH, (b + 1) * CH)
         r = (b % 2) * 2
         got = table[b // 2]
@@ -188,7 +195,10 @@
         ends[:128, at] = jnp.where(hit & (prior < 0), 1.0, 0.0).astype(BF)
         ends[128:, at] = jnp.where(hit & (later >= CH), 1.0, 0.0).astype(BF)
         held.append(jnp.max(jnp.where(hit, 1.0, 0.0), axis=1, keepdims=True))
-    n = len(held)
+        if b == n // 2 - 1:
+            send(near.at[pl.ds(0, n // 2)], near_h.at[pl.ds(0, n // 2)], 0)
+    send(near.at[pl.ds(n // 2, n // 2)], near_h.at[pl.ds(n // 2, n // 2)], 1)
+    send(ends, ends_h, 2)
     before = jnp.zeros((128, 1), F32)
     after = jnp.zeros((128, 1), F32)
     for b in range(n):
@@ -199,6 +209,9 @@
         at = slice(e * CH, (e + 1) * CH)
         tops[128:, at] = (ends[128:, at].astype(F32) * (1.0 - after)).astype(BF)
         after = jnp.maximum(after, held[e])
+    send(tops, tops_h, 3)
+    for copy in copies:
+        copy.wait()
 
 
 def chains(table, rows, after):
@@ -206,11 +219,13 @@
     return call(
         chain_kernel,
         "chains",
-        [shape((n, CH, CH), BF)] + [shape((256, rows), BF)] * 2 + [shape((128, rows), BF)],
+        [pltpu.HBM((n, CH, CH), BF)] + [pltpu.HBM((256, rows), BF)] * 2 + [shape((128, rows), BF)],
         [VMEM],
         (table,),
+        [pltpu.VMEM((n, CH, CH), BF)] + [pltpu.VMEM((256, rows), BF)] * 2 + [pltpu.SemaphoreType.DMA((4,))],
         data=12 * MB,
         after=after,
+        out_specs=[HBM] * 3 + [VMEM],
     )
 
 
@@ -422,50 +437,22 @@
     )
 
 
-def finish_kernel(axis, idx, product, tied, rows_g, keep, s1, s2, s3, ties, acc):
+def finish_kernel(product, tied, rows_g, out, ties):
     for p in range(8):
         at = (p % 2) * 128 + (p // 2) * COLS
         ties[at : at + COLS, :] = tied[p]
-    wide = acc.shape[1]
-    at = slice(0, wide) if axis == "x" else slice(wide, 2 * wide)
-    acc[...] = product[:, at] + jnp.dot(ties[...], rows_g[:, at], preferred_element_type=F32)
-    me = idx[2] if axis == "x" else idx[3]
-    for k, ref in enumerate((keep, s1, s2, s3)):
-        to = lax.rem(me + k, 4)
-        for j in range(4):
-            row = j * 64 + to * 16 if axis == "x" else to * 64 + j * 16
-            ref[j] = acc[pl.ds(pl.multiple_of(row, 16), 16), :].astype(ref.dtype)
-
-
-def finish(axis, idx, product, tied, rows_g, after=()):
-    wide = product.shape[1] // 2
-    return call(
-        functools.partial(finish_kernel, axis),
-        "finish_" + axis,
-        [shape((4, 16, wide), F32)] + [shape((4, 16, wide), BF)] * 3,
-        [SMEM] + [VMEM] * 3,
-        (idx, product, tied, rows_g),
-        [pltpu.VMEM((256, 256), BF), pltpu.VMEM((256, wide), F32)],
-        after=after,
-    )
-
-
-def fold_kernel(which, idx, keep, r1, r2, r3, own, s1, s2, s3):
-    me = idx[which]
-    for k, ref in enumerate((own, s1, s2, s3)):
-        to = lax.rem(me + k, 4)
-        ref[...] = keep[to] + r1[to].astype(F32) + r2[to].astype(F32) + r3[to].astype(F32)
-
-
-def fold(which, idx, keep, recv):
-    wide = keep.shape[2]
-    return call(
-        functools.partial(fold_kernel, which),
-        "fold",
-        [shape((16, wide), F32)] * 4,
-        [SMEM] + [VMEM] * 4,
-        (idx, keep, *recv),
-    )
+    tile = 512
+    for c in range(0, product.shape[1], tile):
+        at = slice(c, c + tile)
+        total = product[:, at] + jnp.dot(ties[...], rows_g[:, at], preferred_element_type=F32)
+        out[:, :, at] = total.reshape(16, 16, tile).astype(BF)
+
+
+def total_kernel(parts, out):
+    total = parts[0].astype(F32)
+    for j in range(1, parts.shape[0]):
+        total = total + parts[j].astype(F32)
+    out[...] = total
 
 
 def y_shift(v, k):
@@ -517,15 +504,16 @@
     pieces = pieces + [core_swap(p) for p in pieces]
     product = adjoint(idx, pieces, green, blocks, after=(tied,))
     tied = exchange(tied, "par")
-    half0 = finish("x", idx, product, tied, rows_g)
-    half1 = finish("z", idx, product, tied, rows_g, after=(half0[1],))
-
-    outs = []
-    for (keep, *sends), one, two, which in ((half0, x_shift, z_shift, 3), (half1, z_shift, x_shift, 2)):
-        last, *sends = fold(which, idx, keep, spread(one, sends))
-        got = spread(two, sends)
-        outs.append(last + got[0] + got[1] + got[2])
-    return jnp.concatenate(outs, axis=1)
+    wide = green.shape[1]
+    parts = call(
+        finish_kernel,
+        "finish",
+        shape((16, 16, wide), BF),
+        [VMEM] * 3,
+        (product, tied, rows_g),
+        [pltpu.VMEM((256, 256), BF)],
+    )
+    return call(total_kernel, "total", shape((16, wide), F32), [VMEM], (exchange(parts, "obs"),))
 
 
 def solution(mesh):

time: 115 us -> 111 us (0.965)
  blocking collectives: 9.88 us -> 34.9 us
  starting transfers between devices: 48.2 us -> 24.9 us
  local copies, waits for them, and re-layouts: 6.43 us -> 2.35 us
    all_to_all x1 -> x2, blocking collectives: 9.88 us -> 34.9 us  [exchange(): return lax.all_to_all(v, axes, split_axis=0, concat_axis=0, tiled=True)]
    ppermute x12 -> x0, starting transfers between devices: 21.6 us -> none  [the longest x6 11 us: z_shift(): lax.ppermute(v, 'obs', [(4 * z + x, 4 * ((z + k) % 4) + x) for z in range...]
    unnamed x28 -> x22, local copies, waits for them, and re-layouts: 6.43 us -> 2.35 us
    ppermute x12 -> x0, waiting for transfers between devices: 3.17 us -> none  [the longest x6 2.83 us: z_shift(): lax.ppermute(v, 'obs', [(4 * z + x, 4 * ((z + k) % 4) + x) for z in range...]
    all_to_all x3, waiting for transfers between devices: 0.01 us -> 1.88 us  [exchange(): return lax.all_to_all(v, axes, split_axis=0, concat_axis=0, tiled=True)]
    all_to_all x3, starting transfers between devices: 18.5 us -> 16.8 us  [exchange(): return lax.all_to_all(v, axes, split_axis=0, concat_axis=0, tiled=True)]
    pallas_call x14 -> x12, Pallas kernels: 41.4 us -> 41.1 us  [call(): pl.pallas_call(body, out_shape=out_shape, in_specs=in_specs + [pl.BlockSp...]
  transfers between devices with their start and end apart: 26 -> 14, of which waited for: 7 -> 3; matrix products, arithmetic and copies ran while one was open for 0% -> 0% of each run, Pallas kernels for 21% -> 22%
where the time goes in v3:
time: 111 us
  Pallas kernels  41.1 us (37%)
  blocking collectives  34.9 us (31%)
  starting transfers between devices  24.9 us (22%)
  waiting for transfers between devices  5.85 us (5%)
  local copies, waits for them, and re-layouts  2.35 us (2%)
  between operations  1.58 us (1%)
    pallas_call x12, Pallas kernels, call(): pl.pallas_call(body, out_shape=out_shape, in_specs=in_specs + [pl.BlockSp...  41.1 us
    all_to_all x2, blocking collectives, exchange(): return lax.all_to_all(v, axes, split_axis=0, concat_axis=0, tiled=True)  34.9 us
    all_to_all x3, starting transfers between devices, exchange(): return lax.all_to_all(v, axes, split_axis=0, concat_axis=0, tiled=True)  16.8 us
    ppermute x6, starting transfers between devices, y_shift(): lax.ppermute(v, 'par', [(2 * y + c, 2 * ((y + k) % 4) + c) for y in range...  7.72 us
    ppermute x6, waiting for transfers between devices, y_shift(): lax.ppermute(v, 'par', [(2 * y + c, 2 * ((y + k) % 4) + c) for y in range...  3.96 us
    unnamed x22, local copies, waits for them, and re-layouts  2.35 us
  transfers between devices with their start and end apart: 14, of which 3 were waited for; matrix products, arithmetic and copies ran while one was open for 0% of the time, Pallas kernels for 22%

profile of v3, /device:TPU:0, one launch (start us, length us, event | category | flops | bytes accessed | tf_op | source)
XLA Modules:
  0.0 110.8 jit_solution(9828181460789660707)
XLA Ops:
  1.3 0.1 pad_add_fusion.refs_0_
  1.4 0.0 copy-start.2
  1.4 0.7 copy-done.2
  2.1 0.6 info.1.refs_4_
  2.6 10.0 %forward.1 = (f32[128,4096]{1,0:T(8,128)S(1)}, f32[128,4096]{1,0:T(8,128)S(1)}) custom-call(s32[4]{0:T(128)S(1)} %pad_add_fusion.refs_0_, bf16[4096,2048]{1,0:T(8,128)(2,1)} %refs_9_.1, s32[16,32]{1,0:T(8,128)} %bitcast.11, bf16[2048,256]{1,0:T(8,128)(2,1)} %refs_3_.1, f32[8,8,128]{2,1,0:T(8,128)S(1)} %info.1.refs_4_), custom_call_target="tpu_custom_call" | custom-call | flops 4294967296 | bytes 16777216 | tf_op jit(solution)/shard_map/forward/pallas_call | solution.py:35
  12.6 0.1 collective-permute-start
  12.7 9.9 %all_to_all.25.refs_0_ = f32[8,8,128]{2,1,0:T(8,128)S(1)} all-to-all(f32[8,8,128]{2,1,0:T(8,128)S(1)} %info.1.refs_4_), channel_id=1, replica_groups=mesh['obs'=16,'par'=8] {'par'}, dimensions={0} | all-to-all | bytes 65536 | tf_op jit(solution)/shard_map/all_to_all | solution.py:475
  22.6 0.6 params.1.refs_3_
  23.3 0.0 collective-permute-done.refs_2_
  23.3 0.7 core_sum.1
  24.0 0.0 copy-start
  24.0 0.6 collective-permute-start.1
  24.6 2.1 %collective-permute-start.2 = (bf16[32,4096]{1,0:T(8,128)(2,1)S(1)}, bf16[32,4096]{1,0:T(8,128)(2,1)S(1)}, u32[]{:S(2)}, u32[]{:S(2)}) collective-permute-start(bf16[32,4096]{1,0:T(8,128)(2,1)S(1)} %get-tuple-element.23), channel_id=1, source_target_pairs={{0,4},{1,5},{2,6},{3,7},{4,0},{5,1},{6,2},{7,3},{8,12},{9,13},{10,... | collective-permute-start | bytes 786440 | tf_op jit(solution)/shard_map/ppermute | solution.py:459
  26.7 1.1 collective-permute-start.3
  27.8 7.9 %all-to-all-start.1 = ((f32[16,8,128]{2,1,0:T(8,128)}), f32[16,8,128]{2,1,0:T(8,128)S(1)}, u32[]{:S(2)}, u32[]{:S(2)}) async-start(f32[16,8,128]{2,1,0:T(8,128)} %params.1.refs_3_), calls=%async_computation.1 | async-start | bytes 131072 | tf_op jit(solution)/shard_map/all_to_all | solution.py:475
  35.7 5.8 %chains.1 = (bf16[16,256,256]{2,1,0:T(8,128)(2,1)}, bf16[256,4096]{1,0:T(8,128)(2,1)}, bf16[256,4096]{1,0:T(8,128)(2,1)}, bf16[128,4096]{1,0:T(8,128)(2,1)S(1)}) custom-call(f32[8,8,128]{2,1,0:T(8,128)S(1)} %all_to_all.25.refs_0_, f32[32,4096]{1,0:T(8,128)S(1)} %get-tuple-element.21.refs_1_.refs_0_), custom_call_target="tpu_custom_call" | custom-call | bytes 12582912 | tf_op jit(solution)/shard_map/chains/pallas_call | solution.py:35
  41.5 1.9 %all-to-all-done.1.refs_0_ = f32[16,8,128]{2,1,0:T(8,128)S(1)} async-done(((f32[16,8,128]{2,1,0:T(8,128)}), f32[16,8,128]{2,1,0:T(8,128)S(1)}, u32[]{:S(2)}, u32[]{:S(2)}) %all-to-all-start.1) | async-done | bytes 65568 | tf_op jit(solution)/shard_map/all_to_all | solution.py:475
  43.3 0.3 coefs.1
  43.6 0.0 collective-permute-done.1.refs_1_
  43.6 0.0 copy-start.8
  43.6 0.0 collective-permute-done.2.refs_2_
  43.7 0.0 copy-start.9
  43.7 0.0 collective-permute-done.3.refs_3_
  43.7 0.0 copy-start.10
  43.7 0.8 copy-done.10
  44.5 0.0 copy-done
  44.5 0.0 copy-done.8
  44.5 0.1 copy-done.9
  44.6 3.7 %group_rows.1 = (bf16[32,4096]{1,0:T(8,128)(2,1)S(1)}, bf16[16,96,128]{2,1,0:T(8,128)(2,1)}) custom-call(f32[32,4096]{1,0:T(8,128)} %copy-done, bf16[32,4096]{1,0:T(8,128)(2,1)} %copy-done.8, bf16[32,4096]{1,0:T(8,128)(2,1)} %copy-done.9, bf16[32,4096]{1,0:T(8,128)(2,1)} %copy-done.10, bf16[16,256,256]{2,1,0:T(8,128)(2,1)} %get-tuple-element.25.refs_4_, ...), custom_call_target="tpu_custom_call" | custom-call | tf_op jit(solution)/shard_map/group_rows/pallas_call | solution.py:35
  48.3 0.0 copy-start.1
  48.3 1.0 collective-permute-start.6
  49.3 2.1 %collective-permute-start.5 = (bf16[32,4096]{1,0:T(8,128)(2,1)S(1)}, bf16[32,4096]{1,0:T(8,128)(2,1)S(1)}, u32[]{:S(2)}, u32[]{:S(2)}) collective-permute-start(bf16[32,4096]{1,0:T(8,128)(2,1)S(1)} %get-tuple-element.29.refs_3_.refs_1_), channel_id=1, source_target_pairs={{0,4},{1,5},{2,6},{3,7},{4,0},{5,1},{6,2},{7,3},{8,12},{9,13},{10,... | collective-permute-start | bytes 786440 | tf_op jit(solution)/shard_map/ppermute | solution.py:459
  51.4 0.9 collective-permute-start.4
  52.2 0.0 collective-permute-start.7
  52.2 5.3 %all-to-all-start.2 = ((bf16[16,96,128]{2,1,0:T(8,128)(2,1)}), bf16[16,96,128]{2,1,0:T(8,128)(2,1)S(1)}, u32[]{:S(2)}, u32[]{:S(2)}) async-start(bf16[16,96,128]{2,1,0:T(8,128)(2,1)} %get-tuple-element.31), calls=%async_computation.2 | async-start | bytes 786432 | tf_op jit(solution)/shard_map/all_to_all | solution.py:475
  57.6 0.0 collective-permute-done.6.refs_4_
  57.6 0.0 copy-start.3
  57.6 0.3 collective-permute-start.10
  57.9 1.2 %collective-permute-done.5.refs_3_ = bf16[32,4096]{1,0:T(8,128)(2,1)S(1)} collective-permute-done((bf16[32,4096]{1,0:T(8,128)(2,1)S(1)}, bf16[32,4096]{1,0:T(8,128)(2,1)S(1)}, u32[]{:S(2)}, u32[]{:S(2)}) %collective-permute-start.5) | collective-permute-done | bytes 262176 | tf_op jit(solution)/shard_map/ppermute | solution.py:459
  59.1 0.0 copy-start.4
  59.1 0.0 collective-permute-start.9
  59.1 2.7 %collective-permute-done.4.refs_2_ = bf16[32,4096]{1,0:T(8,128)(2,1)S(1)} collective-permute-done((bf16[32,4096]{1,0:T(8,128)(2,1)S(1)}, bf16[32,4096]{1,0:T(8,128)(2,1)S(1)}, u32[]{:S(2)}, u32[]{:S(2)}) %collective-permute-start.4) | collective-permute-done | bytes 262176 | tf_op jit(solution)/shard_map/ppermute | solution.py:459
  61.9 0.0 collective-permute-start.8
  61.9 8.3 %end_rows.1.refs_3_.refs_2_ = bf16[256,2048]{1,0:T(8,128)(2,1)S(1)} custom-call(bf16[4096,2048]{1,0:T(8,128)(2,1)} %refs_9_.1, s32[16,32]{1,0:T(8,128)} %bitcast.12, bf16[256,4096]{1,0:T(8,128)(2,1)} %get-tuple-element.32.refs_2_, bf16[32,4096]{1,0:T(8,128)(2,1)S(1)} %get-tuple-element.29.refs_3_.refs_1_), custom_call_target="tpu_custom_call" | custom-call | flops 4294967296 | bytes 16777216 | tf_op jit(solution)/shard_map/end_rows/pallas_call | solution.py:35
  70.1 0.0 copy-done.1
  70.1 0.0 copy-done.3
  70.2 0.0 copy-done.4
  70.2 0.0 copy-done.5
  70.2 0.0 all-to-all-done.2.refs_2_
  70.2 1.3 %tie.1.refs_11_ = bf16[8,32,256]{2,1,0:T(8,128)(2,1)} custom-call(s32[4]{0:T(128)S(1)} %pad_add_fusion.refs_0_, f32[8,128]{1,0:T(8,128)S(1)} %get-tuple-element.30.refs_1_, bf16[16,96,128]{2,1,0:T(8,128)(2,1)S(1)} %all-to-all-done.2.refs_2_, bf16[256,2048]{1,0:T(8,128)(2,1)S(1)} %end_rows.1.refs_3_.refs_2_), custom_call_target="tpu_custom_call" | custom-call | tf_op jit(solution)/shard_map/tie/pallas_call | solution.py:35
  71.5 3.6 %all-to-all-start.3 = ((bf16[8,32,256]{2,1,0:T(8,128)(2,1)}), bf16[8,32,256]{2,1,0:T(8,128)(2,1)S(1)}, u32[]{:S(2)}, u32[]{:S(2)}) async-start(bf16[8,32,256]{2,1,0:T(8,128)(2,1)} %tie.1.refs_11_), calls=%async_computation.3 | async-start | bytes 262144 | tf_op jit(solution)/shard_map/all_to_all | solution.py:475
  75.1 0.0 collective-permute-done.7.refs_5_
  75.1 0.0 copy-start.6
  75.1 0.0 collective-permute-done.10.refs_8_
  75.1 0.0 copy-start.7
  75.1 0.0 collective-permute-done.9.refs_7_
  75.1 0.7 copy-done.6
  75.8 0.1 copy-done.7
  75.9 0.0 collective-permute-done.8.refs_6_
  75.9 8.6 %adjoint.1.refs_0_ = f32[256,2048]{1,0:T(8,128)S(1)} custom-call(s32[4]{0:T(128)S(1)} %pad_add_fusion.refs_0_, bf16[32,4096]{1,0:T(8,128)(2,1)} %copy-done.1, bf16[32,4096]{1,0:T(8,128)(2,1)} %copy-done.5, bf16[32,4096]{1,0:T(8,128)(2,1)} %copy-done.4, bf16[32,4096]{1,0:T(8,128)(2,1)} %copy-done.3, bf16[32,4096]{1,0:T(8,128)(2,1)} %copy-done.6, ...), custom_call_target="tpu_custom_call" | custom-call | flops 4294967296 | bytes 16777216 | tf_op jit(solution)/shard_map/adjoint/pallas_call | solution.py:35
  84.5 0.0 all-to-all-done.3.refs_1_
  84.5 0.4 finish.1
  85.0 25.1 %all_to_all.26.refs_0_ = bf16[16,16,2048]{2,1,0:T(8,128)(2,1)S(1)} all-to-all(bf16[16,16,2048]{2,1,0:T(8,128)(2,1)S(1)} %finish.1), channel_id=1, replica_groups=mesh['obs'=16,'par'=8] {'obs'}, dimensions={0} | all-to-all | bytes 2097152 | tf_op jit(solution)/shard_map/all_to_all | solution.py:475
  110.0 0.8 total.1
  (1 shorter events, 0.0 us)
Async XLA Ops:
  1.4 0.7 copy-start.2
  12.6 10.6 %collective-permute-start = (f32[128,4096]{1,0:T(8,128)S(1)}, f32[128,4096]{1,0:T(8,128)S(1)}, u32[]{:S(2)}, u32[]{:S(2)}) collective-permute-start(f32[128,4096]{1,0:T(8,128)S(1)} %get-tuple-element.20.refs_1_), channel_id=1, source_target_pairs={{0,1},{1,0},{2,3},{3,2},{4,5},{5,4},{6,7},{7,6},{8,9},{9,8},{10,11... | collective-permute-start | bytes 6291464 | tf_op jit(solution)/shard_map/ppermute | solution.py:463
  24.0 20.5 %copy-start = (f32[32,4096]{1,0:T(8,128)}, f32[32,4096]{1,0:T(8,128)S(1)}, u32[]{:S(2)}) copy-start(f32[32,4096]{1,0:T(8,128)S(1)} %get-tuple-element.21.refs_1_.refs_0_) | copy-start | bytes 1572868
  24.0 19.6 %collective-permute-start.1 = (bf16[32,4096]{1,0:T(8,128)(2,1)S(1)}, bf16[32,4096]{1,0:T(8,128)(2,1)S(1)}, u32[]{:S(2)}, u32[]{:S(2)}) collective-permute-start(bf16[32,4096]{1,0:T(8,128)(2,1)S(1)} %get-tuple-element.22), channel_id=1, source_target_pairs={{0,2},{1,3},{2,4},{3,5},{4,6},{5,7},{6,0},{7,1},{8,10},{9,11},{10,... | collective-permute-start | bytes 786440 | tf_op jit(solution)/shard_map/ppermute | solution.py:459
  24.6 19.0 %collective-permute-start.2 = (bf16[32,4096]{1,0:T(8,128)(2,1)S(1)}, bf16[32,4096]{1,0:T(8,128)(2,1)S(1)}, u32[]{:S(2)}, u32[]{:S(2)}) collective-permute-start(bf16[32,4096]{1,0:T(8,128)(2,1)S(1)} %get-tuple-element.23), channel_id=1, source_target_pairs={{0,4},{1,5},{2,6},{3,7},{4,0},{5,1},{6,2},{7,3},{8,12},{9,13},{10,... | collective-permute-start | bytes 786440 | tf_op jit(solution)/shard_map/ppermute | solution.py:459
  26.7 17.0 %collective-permute-start.3 = (bf16[32,4096]{1,0:T(8,128)(2,1)S(1)}, bf16[32,4096]{1,0:T(8,128)(2,1)S(1)}, u32[]{:S(2)}, u32[]{:S(2)}) collective-permute-start(bf16[32,4096]{1,0:T(8,128)(2,1)S(1)} %get-tuple-element.24), channel_id=1, source_target_pairs={{0,6},{1,7},{2,0},{3,1},{4,2},{5,3},{6,4},{7,5},{8,14},{9,15},{10,... | collective-permute-start | bytes 786440 | tf_op jit(solution)/shard_map/ppermute | solution.py:459
  27.8 15.5 %all-to-all-start.1 = ((f32[16,8,128]{2,1,0:T(8,128)}), f32[16,8,128]{2,1,0:T(8,128)S(1)}, u32[]{:S(2)}, u32[]{:S(2)}) async-start(f32[16,8,128]{2,1,0:T(8,128)} %params.1.refs_3_), calls=%async_computation.1 | async-start | bytes 131072 | tf_op jit(solution)/shard_map/all_to_all | solution.py:475
  43.6 0.9 copy-start.8
  43.7 0.9 copy-start.9
  43.7 0.8 copy-start.10
  48.3 21.9 %copy-start.1 = (bf16[32,4096]{1,0:T(8,128)(2,1)}, bf16[32,4096]{1,0:T(8,128)(2,1)S(1)}, u32[]{:S(2)}) copy-start(bf16[32,4096]{1,0:T(8,128)(2,1)S(1)} %get-tuple-element.29.refs_3_.refs_1_) | copy-start | bytes 786436
  48.3 9.3 %collective-permute-start.6 = (bf16[32,4096]{1,0:T(8,128)(2,1)S(1)}, bf16[32,4096]{1,0:T(8,128)(2,1)S(1)}, u32[]{:S(2)}, u32[]{:S(2)}) collective-permute-start(bf16[32,4096]{1,0:T(8,128)(2,1)S(1)} %get-tuple-element.29.refs_3_.refs_1_), channel_id=1, source_target_pairs={{0,6},{1,7},{2,0},{3,1},{4,2},{5,3},{6,4},{7,5},{8,14},{9,15},{10,... | collective-permute-start | bytes 786440 | tf_op jit(solution)/shard_map/ppermute | solution.py:459
  49.3 9.8 %collective-permute-start.5 = (bf16[32,4096]{1,0:T(8,128)(2,1)S(1)}, bf16[32,4096]{1,0:T(8,128)(2,1)S(1)}, u32[]{:S(2)}, u32[]{:S(2)}) collective-permute-start(bf16[32,4096]{1,0:T(8,128)(2,1)S(1)} %get-tuple-element.29.refs_3_.refs_1_), channel_id=1, source_target_pairs={{0,4},{1,5},{2,6},{3,7},{4,0},{5,1},{6,2},{7,3},{8,12},{9,13},{10,... | collective-permute-start | bytes 786440 | tf_op jit(solution)/shard_map/ppermute | solution.py:459
  51.4 10.5 %collective-permute-start.4 = (bf16[32,4096]{1,0:T(8,128)(2,1)S(1)}, bf16[32,4096]{1,0:T(8,128)(2,1)S(1)}, u32[]{:S(2)}, u32[]{:S(2)}) collective-permute-start(bf16[32,4096]{1,0:T(8,128)(2,1)S(1)} %get-tuple-element.29.refs_3_.refs_1_), channel_id=1, source_target_pairs={{0,2},{1,3},{2,4},{3,5},{4,6},{5,7},{6,0},{7,1},{8,10},{9,11},{10,... | collective-permute-start | bytes 786440 | tf_op jit(solution)/shard_map/ppermute | solution.py:459
  52.2 22.9 %collective-permute-start.7 = (bf16[32,4096]{1,0:T(8,128)(2,1)S(1)}, bf16[32,4096]{1,0:T(8,128)(2,1)S(1)}, u32[]{:S(2)}, u32[]{:S(2)}) collective-permute-start(bf16[32,4096]{1,0:T(8,128)(2,1)S(1)} %get-tuple-element.29.refs_3_.refs_1_), channel_id=1, source_target_pairs={{0,1},{1,0},{2,3},{3,2},{4,5},{5,4},{6,7},{7,6},{8,9},{9,8},{10,11... | collective-permute-start | bytes 786440 | tf_op jit(solution)/shard_map/ppermute | solution.py:463
  52.2 18.0 %all-to-all-start.2 = ((bf16[16,96,128]{2,1,0:T(8,128)(2,1)}), bf16[16,96,128]{2,1,0:T(8,128)(2,1)S(1)}, u32[]{:S(2)}, u32[]{:S(2)}) async-start(bf16[16,96,128]{2,1,0:T(8,128)(2,1)} %get-tuple-element.31), calls=%async_computation.2 | async-start | bytes 786432 | tf_op jit(solution)/shard_map/all_to_all | solution.py:475
  57.6 12.6 %copy-start.3 = (bf16[32,4096]{1,0:T(8,128)(2,1)}, bf16[32,4096]{1,0:T(8,128)(2,1)S(1)}, u32[]{:S(2)}) copy-start(bf16[32,4096]{1,0:T(8,128)(2,1)S(1)} %collective-permute-done.6.refs_4_) | copy-start | bytes 786436
  57.6 17.5 %collective-permute-start.10 = (bf16[32,4096]{1,0:T(8,128)(2,1)S(1)}, bf16[32,4096]{1,0:T(8,128)(2,1)S(1)}, u32[]{:S(2)}, u32[]{:S(2)}) collective-permute-start(bf16[32,4096]{1,0:T(8,128)(2,1)S(1)} %collective-permute-done.6.refs_4_), channel_id=1, source_target_pairs={{0,1},{1,0},{2,3},{3,2},{4,5},{5,4},{6,7},{7,6},{8,9},{9,8},{10,11... | collective-permute-start | bytes 786440 | tf_op jit(solution)/shard_map/ppermute | solution.py:463
  59.1 11.0 %copy-start.4 = (bf16[32,4096]{1,0:T(8,128)(2,1)}, bf16[32,4096]{1,0:T(8,128)(2,1)S(1)}, u32[]{:S(2)}) copy-start(bf16[32,4096]{1,0:T(8,128)(2,1)S(1)} %collective-permute-done.5.refs_3_) | copy-start | bytes 786436
  59.1 16.0 %collective-permute-start.9 = (bf16[32,4096]{1,0:T(8,128)(2,1)S(1)}, bf16[32,4096]{1,0:T(8,128)(2,1)}, u32[]{:S(2)}, u32[]{:S(2)}) collective-permute-start(bf16[32,4096]{1,0:T(8,128)(2,1)S(1)} %collective-permute-done.5.refs_3_), channel_id=1, source_target_pairs={{0,1},{1,0},{2,3},{3,2},{4,5},{5,4},{6,7},{7,6},{8,9},{9,8},{10,11... | collective-permute-start | bytes 786440 | tf_op jit(solution)/shard_map/ppermute | solution.py:463
  61.9 8.3 %copy-start.5 = (bf16[32,4096]{1,0:T(8,128)(2,1)}, bf16[32,4096]{1,0:T(8,128)(2,1)S(1)}, u32[]{:S(2)}) copy-start(bf16[32,4096]{1,0:T(8,128)(2,1)S(1)} %collective-permute-done.4.refs_2_) | copy-start | bytes 786436
  61.9 14.0 %collective-permute-start.8 = (bf16[32,4096]{1,0:T(8,128)(2,1)S(1)}, bf16[32,4096]{1,0:T(8,128)(2,1)}, u32[]{:S(2)}, u32[]{:S(2)}) collective-permute-start(bf16[32,4096]{1,0:T(8,128)(2,1)S(1)} %collective-permute-done.4.refs_2_), channel_id=1, source_target_pairs={{0,1},{1,0},{2,3},{3,2},{4,5},{5,4},{6,7},{7,6},{8,9},{9,8},{10,11... | collective-permute-start | bytes 786440 | tf_op jit(solution)/shard_map/ppermute | solution.py:463
  71.5 13.0 %all-to-all-start.3 = ((bf16[8,32,256]{2,1,0:T(8,128)(2,1)}), bf16[8,32,256]{2,1,0:T(8,128)(2,1)S(1)}, u32[]{:S(2)}, u32[]{:S(2)}) async-start(bf16[8,32,256]{2,1,0:T(8,128)(2,1)} %tie.1.refs_11_), calls=%async_computation.3 | async-start | bytes 262144 | tf_op jit(solution)/shard_map/all_to_all | solution.py:475
  75.1 0.7 copy-start.6
  75.1 0.8 copy-start.7

commit v4 on v3

--- a/solution.py
+++ b/solution.py
@@ -80,7 +80,7 @@
     ]
     for copy in small:
         copy.start()
-    for i in range(2):
+    for i in range(3):
         fetch(green, 0, buf, sem, i).start()
     small[0].wait()
     expand(own_blocks, gate)
@@ -90,8 +90,8 @@
         panel[pl.ds(at, 128), :] = own_probes[:, part * 128 : (part + 1) * 128].T
     for i in range(steps):
         fetch(green, 0, buf, sem, i).wait()
-        if i + 2 < steps:
-            fetch(green, 0, buf, sem, i + 2).start()
+        if i + 3 < steps:
+            fetch(green, 0, buf, sem, i + 3).start()
         mask_rows(buf, gate, i, tile, 0)
         at = slice(i * tile, (i + 1) * tile)
         part = lax.dot_general(panel[...], buf[at, :], NT, preferred_element_type=F32)
@@ -113,7 +113,7 @@
             pltpu.VMEM(probes.shape, BF),
             pltpu.VMEM((256, par_dev), BF),
             pltpu.VMEM((rows // BLK, par_dev), F32),
-            pltpu.SemaphoreType.DMA((8,)),
+            pltpu.SemaphoreType.DMA((16,)),
             pltpu.SemaphoreType.DMA((2,)),
         ],
         flops=2 * rows * par_dev * 256,

time: 111 us -> 116 us (1.045)
  Pallas kernels: 41.1 us -> 45.9 us
    pallas_call x12, Pallas kernels: 41.1 us -> 45.9 us  [call(): pl.pallas_call(body, out_shape=out_shape, in_specs=in_specs + [pl.BlockSp...]
  transfers between devices with their start and end apart: 14 -> 14, of which waited for: 3 -> 3; matrix products, arithmetic and copies ran while one was open for 0% -> 0% of each run, Pallas kernels for 22% -> 21%
where the time goes in v4:
time: 116 us
  Pallas kernels  45.9 us (40%)
  blocking collectives  34.9 us (30%)
  starting transfers between devices  24.9 us (21%)
  waiting for transfers between devices  5.86 us (5%)
  local copies, waits for them, and re-layouts  2.35 us (2%)
  between operations  1.58 us (1%)
    pallas_call x12, Pallas kernels, call(): pl.pallas_call(body, out_shape=out_shape, in_specs=in_specs + [pl.BlockSp...  45.9 us
    all_to_all x2, blocking collectives, exchange(): return lax.all_to_all(v, axes, split_axis=0, concat_axis=0, tiled=True)  34.9 us
    all_to_all x3, starting transfers between devices, exchange(): return lax.all_to_all(v, axes, split_axis=0, concat_axis=0, tiled=True)  16.8 us
    ppermute x6, starting transfers between devices, y_shift(): lax.ppermute(v, 'par', [(2 * y + c, 2 * ((y + k) % 4) + c) for y in range...  7.72 us
    ppermute x6, waiting for transfers between devices, y_shift(): lax.ppermute(v, 'par', [(2 * y + c, 2 * ((y + k) % 4) + c) for y in range...  3.96 us
    unnamed x22, local copies, waits for them, and re-layouts  2.35 us
  transfers between devices with their start and end apart: 14, of which 3 were waited for; matrix products, arithmetic and copies ran while one was open for 0% of the time, Pallas kernels for 21%

profile of v4, /device:TPU:0, one launch (start us, length us, event | category | flops | bytes accessed | tf_op | source)
XLA Modules:
  0.0 115.6 jit_solution(8029454473071086970)
XLA Ops:
  1.3 0.1 pad_add_fusion.refs_0_
  1.4 0.0 copy-start.2
  1.4 0.7 copy-done.2
  2.1 0.6 info.1.refs_4_
  2.6 14.8 %forward.1 = (f32[128,4096]{1,0:T(8,128)S(1)}, f32[128,4096]{1,0:T(8,128)S(1)}) custom-call(s32[4]{0:T(128)S(1)} %pad_add_fusion.refs_0_, bf16[4096,2048]{1,0:T(8,128)(2,1)} %refs_9_.1, s32[16,32]{1,0:T(8,128)} %bitcast.11, bf16[2048,256]{1,0:T(8,128)(2,1)} %refs_3_.1, f32[8,8,128]{2,1,0:T(8,128)S(1)} %info.1.refs_4_), custom_call_target="tpu_custom_call" | custom-call | flops 4294967296 | bytes 16777216 | tf_op jit(solution)/shard_map/forward/pallas_call | solution.py:35
  17.4 0.1 collective-permute-start
  17.5 9.9 %all_to_all.25.refs_0_ = f32[8,8,128]{2,1,0:T(8,128)S(1)} all-to-all(f32[8,8,128]{2,1,0:T(8,128)S(1)} %info.1.refs_4_), channel_id=1, replica_groups=mesh['obs'=16,'par'=8] {'par'}, dimensions={0} | all-to-all | bytes 65536 | tf_op jit(solution)/shard_map/all_to_all | solution.py:475
  27.4 0.6 params.1.refs_3_
  28.0 0.0 collective-permute-done.refs_2_
  28.0 0.7 core_sum.1
  28.8 0.0 copy-start
  28.8 0.6 collective-permute-start.1
  29.4 2.1 %collective-permute-start.2 = (bf16[32,4096]{1,0:T(8,128)(2,1)S(1)}, bf16[32,4096]{1,0:T(8,128)(2,1)S(1)}, u32[]{:S(2)}, u32[]{:S(2)}) collective-permute-start(bf16[32,4096]{1,0:T(8,128)(2,1)S(1)} %get-tuple-element.23), channel_id=1, source_target_pairs={{0,4},{1,5},{2,6},{3,7},{4,0},{5,1},{6,2},{7,3},{8,12},{9,13},{10,... | collective-permute-start | bytes 786440 | tf_op jit(solution)/shard_map/ppermute | solution.py:459
  31.5 1.1 collective-permute-start.3
  32.6 7.9 %all-to-all-start.1 = ((f32[16,8,128]{2,1,0:T(8,128)}), f32[16,8,128]{2,1,0:T(8,128)S(1)}, u32[]{:S(2)}, u32[]{:S(2)}) async-start(f32[16,8,128]{2,1,0:T(8,128)} %params.1.refs_3_), calls=%async_computation.1 | async-start | bytes 131072 | tf_op jit(solution)/shard_map/all_to_all | solution.py:475
  40.5 5.8 %chains.1 = (bf16[16,256,256]{2,1,0:T(8,128)(2,1)}, bf16[256,4096]{1,0:T(8,128)(2,1)}, bf16[256,4096]{1,0:T(8,128)(2,1)}, bf16[128,4096]{1,0:T(8,128)(2,1)S(1)}) custom-call(f32[8,8,128]{2,1,0:T(8,128)S(1)} %all_to_all.25.refs_0_, f32[32,4096]{1,0:T(8,128)S(1)} %get-tuple-element.21.refs_1_.refs_0_), custom_call_target="tpu_custom_call" | custom-call | bytes 12582912 | tf_op jit(solution)/shard_map/chains/pallas_call | solution.py:35
  46.3 1.9 %all-to-all-done.1.refs_0_ = f32[16,8,128]{2,1,0:T(8,128)S(1)} async-done(((f32[16,8,128]{2,1,0:T(8,128)}), f32[16,8,128]{2,1,0:T(8,128)S(1)}, u32[]{:S(2)}, u32[]{:S(2)}) %all-to-all-start.1) | async-done | bytes 65568 | tf_op jit(solution)/shard_map/all_to_all | solution.py:475
  48.1 0.3 coefs.1
  48.4 0.0 collective-permute-done.1.refs_1_
  48.4 0.0 copy-start.8
  48.4 0.0 collective-permute-done.2.refs_2_
  48.5 0.0 copy-start.9
  48.5 0.0 collective-permute-done.3.refs_3_
  48.5 0.0 copy-start.10
  48.5 0.8 copy-done.10
  49.3 0.0 copy-done
  49.3 0.0 copy-done.8
  49.3 0.1 copy-done.9
  49.4 3.7 %group_rows.1 = (bf16[32,4096]{1,0:T(8,128)(2,1)S(1)}, bf16[16,96,128]{2,1,0:T(8,128)(2,1)}) custom-call(f32[32,4096]{1,0:T(8,128)} %copy-done, bf16[32,4096]{1,0:T(8,128)(2,1)} %copy-done.8, bf16[32,4096]{1,0:T(8,128)(2,1)} %copy-done.9, bf16[32,4096]{1,0:T(8,128)(2,1)} %copy-done.10, bf16[16,256,256]{2,1,0:T(8,128)(2,1)} %get-tuple-element.25.refs_4_, ...), custom_call_target="tpu_custom_call" | custom-call | tf_op jit(solution)/shard_map/group_rows/pallas_call | solution.py:35
  53.1 0.0 copy-start.1
  53.1 1.0 collective-permute-start.6
  54.1 2.1 %collective-permute-start.5 = (bf16[32,4096]{1,0:T(8,128)(2,1)S(1)}, bf16[32,4096]{1,0:T(8,128)(2,1)S(1)}, u32[]{:S(2)}, u32[]{:S(2)}) collective-permute-start(bf16[32,4096]{1,0:T(8,128)(2,1)S(1)} %get-tuple-element.29.refs_3_.refs_1_), channel_id=1, source_target_pairs={{0,4},{1,5},{2,6},{3,7},{4,0},{5,1},{6,2},{7,3},{8,12},{9,13},{10,... | collective-permute-start | bytes 786440 | tf_op jit(solution)/shard_map/ppermute | solution.py:459
  56.1 0.9 collective-permute-start.4
  57.0 0.0 collective-permute-start.7
  57.0 5.3 %all-to-all-start.2 = ((bf16[16,96,128]{2,1,0:T(8,128)(2,1)}), bf16[16,96,128]{2,1,0:T(8,128)(2,1)S(1)}, u32[]{:S(2)}, u32[]{:S(2)}) async-start(bf16[16,96,128]{2,1,0:T(8,128)(2,1)} %get-tuple-element.31), calls=%async_computation.2 | async-start | bytes 786432 | tf_op jit(solution)/shard_map/all_to_all | solution.py:475
  62.4 0.0 collective-permute-done.6.refs_4_
  62.4 0.0 copy-start.3
  62.4 0.3 collective-permute-start.10
  62.7 1.2 %collective-permute-done.5.refs_3_ = bf16[32,4096]{1,0:T(8,128)(2,1)S(1)} collective-permute-done((bf16[32,4096]{1,0:T(8,128)(2,1)S(1)}, bf16[32,4096]{1,0:T(8,128)(2,1)S(1)}, u32[]{:S(2)}, u32[]{:S(2)}) %collective-permute-start.5) | collective-permute-done | bytes 262176 | tf_op jit(solution)/shard_map/ppermute | solution.py:459
  63.9 0.0 copy-start.4
  63.9 0.0 collective-permute-start.9
  63.9 2.7 %collective-permute-done.4.refs_2_ = bf16[32,4096]{1,0:T(8,128)(2,1)S(1)} collective-permute-done((bf16[32,4096]{1,0:T(8,128)(2,1)S(1)}, bf16[32,4096]{1,0:T(8,128)(2,1)S(1)}, u32[]{:S(2)}, u32[]{:S(2)}) %collective-permute-start.4) | collective-permute-done | bytes 262176 | tf_op jit(solution)/shard_map/ppermute | solution.py:459
  66.6 0.0 collective-permute-start.8
  66.7 8.3 %end_rows.1.refs_3_.refs_2_ = bf16[256,2048]{1,0:T(8,128)(2,1)S(1)} custom-call(bf16[4096,2048]{1,0:T(8,128)(2,1)} %refs_9_.1, s32[16,32]{1,0:T(8,128)} %bitcast.12, bf16[256,4096]{1,0:T(8,128)(2,1)} %get-tuple-element.32.refs_2_, bf16[32,4096]{1,0:T(8,128)(2,1)S(1)} %get-tuple-element.29.refs_3_.refs_1_), custom_call_target="tpu_custom_call" | custom-call | flops 4294967296 | bytes 16777216 | tf_op jit(solution)/shard_map/end_rows/pallas_call | solution.py:35
  74.9 0.0 copy-done.1
  74.9 0.0 copy-done.3
  74.9 0.0 copy-done.4
  75.0 0.0 copy-done.5
  75.0 0.0 all-to-all-done.2.refs_2_
  75.0 1.3 %tie.1.refs_11_ = bf16[8,32,256]{2,1,0:T(8,128)(2,1)} custom-call(s32[4]{0:T(128)S(1)} %pad_add_fusion.refs_0_, f32[8,128]{1,0:T(8,128)S(1)} %get-tuple-element.30.refs_1_, bf16[16,96,128]{2,1,0:T(8,128)(2,1)S(1)} %all-to-all-done.2.refs_2_, bf16[256,2048]{1,0:T(8,128)(2,1)S(1)} %end_rows.1.refs_3_.refs_2_), custom_call_target="tpu_custom_call" | custom-call | tf_op jit(solution)/shard_map/tie/pallas_call | solution.py:35
  76.3 3.6 %all-to-all-start.3 = ((bf16[8,32,256]{2,1,0:T(8,128)(2,1)}), bf16[8,32,256]{2,1,0:T(8,128)(2,1)S(1)}, u32[]{:S(2)}, u32[]{:S(2)}) async-start(bf16[8,32,256]{2,1,0:T(8,128)(2,1)} %tie.1.refs_11_), calls=%async_computation.3 | async-start | bytes 262144 | tf_op jit(solution)/shard_map/all_to_all | solution.py:475
  79.9 0.0 collective-permute-done.7.refs_5_
  79.9 0.0 copy-start.6
  79.9 0.0 collective-permute-done.10.refs_8_
  79.9 0.0 copy-start.7
  79.9 0.0 collective-permute-done.9.refs_7_
  79.9 0.7 copy-done.6
  80.6 0.1 copy-done.7
  80.7 0.0 collective-permute-done.8.refs_6_
  80.7 8.6 %adjoint.1.refs_0_ = f32[256,2048]{1,0:T(8,128)S(1)} custom-call(s32[4]{0:T(128)S(1)} %pad_add_fusion.refs_0_, bf16[32,4096]{1,0:T(8,128)(2,1)} %copy-done.1, bf16[32,4096]{1,0:T(8,128)(2,1)} %copy-done.5, bf16[32,4096]{1,0:T(8,128)(2,1)} %copy-done.4, bf16[32,4096]{1,0:T(8,128)(2,1)} %copy-done.3, bf16[32,4096]{1,0:T(8,128)(2,1)} %copy-done.6, ...), custom_call_target="tpu_custom_call" | custom-call | flops 4294967296 | bytes 16777216 | tf_op jit(solution)/shard_map/adjoint/pallas_call | solution.py:35
  89.3 0.0 all-to-all-done.3.refs_1_
  89.3 0.4 finish.1
  89.8 25.1 %all_to_all.26.refs_0_ = bf16[16,16,2048]{2,1,0:T(8,128)(2,1)S(1)} all-to-all(bf16[16,16,2048]{2,1,0:T(8,128)(2,1)S(1)} %finish.1), channel_id=1, replica_groups=mesh['obs'=16,'par'=8] {'obs'}, dimensions={0} | all-to-all | bytes 2097152 | tf_op jit(solution)/shard_map/all_to_all | solution.py:475
  114.8 0.8 total.1
  (1 shorter events, 0.0 us)
Async XLA Ops:
  1.4 0.7 copy-start.2
  17.4 10.6 %collective-permute-start = (f32[128,4096]{1,0:T(8,128)S(1)}, f32[128,4096]{1,0:T(8,128)S(1)}, u32[]{:S(2)}, u32[]{:S(2)}) collective-permute-start(f32[128,4096]{1,0:T(8,128)S(1)} %get-tuple-element.20.refs_1_), channel_id=1, source_target_pairs={{0,1},{1,0},{2,3},{3,2},{4,5},{5,4},{6,7},{7,6},{8,9},{9,8},{10,11... | collective-permute-start | bytes 6291464 | tf_op jit(solution)/shard_map/ppermute | solution.py:463
  28.8 20.5 %copy-start = (f32[32,4096]{1,0:T(8,128)}, f32[32,4096]{1,0:T(8,128)S(1)}, u32[]{:S(2)}) copy-start(f32[32,4096]{1,0:T(8,128)S(1)} %get-tuple-element.21.refs_1_.refs_0_) | copy-start | bytes 1572868
  28.8 19.6 %collective-permute-start.1 = (bf16[32,4096]{1,0:T(8,128)(2,1)S(1)}, bf16[32,4096]{1,0:T(8,128)(2,1)S(1)}, u32[]{:S(2)}, u32[]{:S(2)}) collective-permute-start(bf16[32,4096]{1,0:T(8,128)(2,1)S(1)} %get-tuple-element.22), channel_id=1, source_target_pairs={{0,2},{1,3},{2,4},{3,5},{4,6},{5,7},{6,0},{7,1},{8,10},{9,11},{10,... | collective-permute-start | bytes 786440 | tf_op jit(solution)/shard_map/ppermute | solution.py:459
  29.4 19.0 %collective-permute-start.2 = (bf16[32,4096]{1,0:T(8,128)(2,1)S(1)}, bf16[32,4096]{1,0:T(8,128)(2,1)S(1)}, u32[]{:S(2)}, u32[]{:S(2)}) collective-permute-start(bf16[32,4096]{1,0:T(8,128)(2,1)S(1)} %get-tuple-element.23), channel_id=1, source_target_pairs={{0,4},{1,5},{2,6},{3,7},{4,0},{5,1},{6,2},{7,3},{8,12},{9,13},{10,... | collective-permute-start | bytes 786440 | tf_op jit(solution)/shard_map/ppermute | solution.py:459
  31.5 17.0 %collective-permute-start.3 = (bf16[32,4096]{1,0:T(8,128)(2,1)S(1)}, bf16[32,4096]{1,0:T(8,128)(2,1)S(1)}, u32[]{:S(2)}, u32[]{:S(2)}) collective-permute-start(bf16[32,4096]{1,0:T(8,128)(2,1)S(1)} %get-tuple-element.24), channel_id=1, source_target_pairs={{0,6},{1,7},{2,0},{3,1},{4,2},{5,3},{6,4},{7,5},{8,14},{9,15},{10,... | collective-permute-start | bytes 786440 | tf_op jit(solution)/shard_map/ppermute | solution.py:459
  32.6 15.6 %all-to-all-start.1 = ((f32[16,8,128]{2,1,0:T(8,128)}), f32[16,8,128]{2,1,0:T(8,128)S(1)}, u32[]{:S(2)}, u32[]{:S(2)}) async-start(f32[16,8,128]{2,1,0:T(8,128)} %params.1.refs_3_), calls=%async_computation.1 | async-start | bytes 131072 | tf_op jit(solution)/shard_map/all_to_all | solution.py:475
  48.4 0.9 copy-start.8
  48.5 0.9 copy-start.9
  48.5 0.8 copy-start.10
  53.1 21.9 %copy-start.1 = (bf16[32,4096]{1,0:T(8,128)(2,1)}, bf16[32,4096]{1,0:T(8,128)(2,1)S(1)}, u32[]{:S(2)}) copy-start(bf16[32,4096]{1,0:T(8,128)(2,1)S(1)} %get-tuple-element.29.refs_3_.refs_1_) | copy-start | bytes 786436
  53.1 9.3 %collective-permute-start.6 = (bf16[32,4096]{1,0:T(8,128)(2,1)S(1)}, bf16[32,4096]{1,0:T(8,128)(2,1)S(1)}, u32[]{:S(2)}, u32[]{:S(2)}) collective-permute-start(bf16[32,4096]{1,0:T(8,128)(2,1)S(1)} %get-tuple-element.29.refs_3_.refs_1_), channel_id=1, source_target_pairs={{0,6},{1,7},{2,0},{3,1},{4,2},{5,3},{6,4},{7,5},{8,14},{9,15},{10,... | collective-permute-start | bytes 786440 | tf_op jit(solution)/shard_map/ppermute | solution.py:459
  54.1 9.8 %collective-permute-start.5 = (bf16[32,4096]{1,0:T(8,128)(2,1)S(1)}, bf16[32,4096]{1,0:T(8,128)(2,1)S(1)}, u32[]{:S(2)}, u32[]{:S(2)}) collective-permute-start(bf16[32,4096]{1,0:T(8,128)(2,1)S(1)} %get-tuple-element.29.refs_3_.refs_1_), channel_id=1, source_target_pairs={{0,4},{1,5},{2,6},{3,7},{4,0},{5,1},{6,2},{7,3},{8,12},{9,13},{10,... | collective-permute-start | bytes 786440 | tf_op jit(solution)/shard_map/ppermute | solution.py:459
  56.1 10.5 %collective-permute-start.4 = (bf16[32,4096]{1,0:T(8,128)(2,1)S(1)}, bf16[32,4096]{1,0:T(8,128)(2,1)S(1)}, u32[]{:S(2)}, u32[]{:S(2)}) collective-permute-start(bf16[32,4096]{1,0:T(8,128)(2,1)S(1)} %get-tuple-element.29.refs_3_.refs_1_), channel_id=1, source_target_pairs={{0,2},{1,3},{2,4},{3,5},{4,6},{5,7},{6,0},{7,1},{8,10},{9,11},{10,... | collective-permute-start | bytes 786440 | tf_op jit(solution)/shard_map/ppermute | solution.py:459
  57.0 22.9 %collective-permute-start.7 = (bf16[32,4096]{1,0:T(8,128)(2,1)S(1)}, bf16[32,4096]{1,0:T(8,128)(2,1)S(1)}, u32[]{:S(2)}, u32[]{:S(2)}) collective-permute-start(bf16[32,4096]{1,0:T(8,128)(2,1)S(1)} %get-tuple-element.29.refs_3_.refs_1_), channel_id=1, source_target_pairs={{0,1},{1,0},{2,3},{3,2},{4,5},{5,4},{6,7},{7,6},{8,9},{9,8},{10,11... | collective-permute-start | bytes 786440 | tf_op jit(solution)/shard_map/ppermute | solution.py:463
  57.0 18.0 %all-to-all-start.2 = ((bf16[16,96,128]{2,1,0:T(8,128)(2,1)}), bf16[16,96,128]{2,1,0:T(8,128)(2,1)S(1)}, u32[]{:S(2)}, u32[]{:S(2)}) async-start(bf16[16,96,128]{2,1,0:T(8,128)(2,1)} %get-tuple-element.31), calls=%async_computation.2 | async-start | bytes 786432 | tf_op jit(solution)/shard_map/all_to_all | solution.py:475
  62.4 12.6 %copy-start.3 = (bf16[32,4096]{1,0:T(8,128)(2,1)}, bf16[32,4096]{1,0:T(8,128)(2,1)S(1)}, u32[]{:S(2)}) copy-start(bf16[32,4096]{1,0:T(8,128)(2,1)S(1)} %collective-permute-done.6.refs_4_) | copy-start | bytes 786436
  62.4 17.5 %collective-permute-start.10 = (bf16[32,4096]{1,0:T(8,128)(2,1)S(1)}, bf16[32,4096]{1,0:T(8,128)(2,1)S(1)}, u32[]{:S(2)}, u32[]{:S(2)}) collective-permute-start(bf16[32,4096]{1,0:T(8,128)(2,1)S(1)} %collective-permute-done.6.refs_4_), channel_id=1, source_target_pairs={{0,1},{1,0},{2,3},{3,2},{4,5},{5,4},{6,7},{7,6},{8,9},{9,8},{10,11... | collective-permute-start | bytes 786440 | tf_op jit(solution)/shard_map/ppermute | solution.py:463
  63.9 11.0 %copy-start.4 = (bf16[32,4096]{1,0:T(8,128)(2,1)}, bf16[32,4096]{1,0:T(8,128)(2,1)S(1)}, u32[]{:S(2)}) copy-start(bf16[32,4096]{1,0:T(8,128)(2,1)S(1)} %collective-permute-done.5.refs_3_) | copy-start | bytes 786436
  63.9 16.0 %collective-permute-start.9 = (bf16[32,4096]{1,0:T(8,128)(2,1)S(1)}, bf16[32,4096]{1,0:T(8,128)(2,1)}, u32[]{:S(2)}, u32[]{:S(2)}) collective-permute-start(bf16[32,4096]{1,0:T(8,128)(2,1)S(1)} %collective-permute-done.5.refs_3_), channel_id=1, source_target_pairs={{0,1},{1,0},{2,3},{3,2},{4,5},{5,4},{6,7},{7,6},{8,9},{9,8},{10,11... | collective-permute-start | bytes 786440 | tf_op jit(solution)/shard_map/ppermute | solution.py:463
  66.6 8.3 %copy-start.5 = (bf16[32,4096]{1,0:T(8,128)(2,1)}, bf16[32,4096]{1,0:T(8,128)(2,1)S(1)}, u32[]{:S(2)}) copy-start(bf16[32,4096]{1,0:T(8,128)(2,1)S(1)} %collective-permute-done.4.refs_2_) | copy-start | bytes 786436
  66.6 14.0 %collective-permute-start.8 = (bf16[32,4096]{1,0:T(8,128)(2,1)S(1)}, bf16[32,4096]{1,0:T(8,128)(2,1)}, u32[]{:S(2)}, u32[]{:S(2)}) collective-permute-start(bf16[32,4096]{1,0:T(8,128)(2,1)S(1)} %collective-permute-done.4.refs_2_), channel_id=1, source_target_pairs={{0,1},{1,0},{2,3},{3,2},{4,5},{5,4},{6,7},{7,6},{8,9},{9,8},{10,11... | collective-permute-start | bytes 786440 | tf_op jit(solution)/shard_map/ppermute | solution.py:463
  76.3 13.0 %all-to-all-start.3 = ((bf16[8,32,256]{2,1,0:T(8,128)(2,1)}), bf16[8,32,256]{2,1,0:T(8,128)(2,1)S(1)}, u32[]{:S(2)}, u32[]{:S(2)}) async-start(bf16[8,32,256]{2,1,0:T(8,128)(2,1)} %tie.1.refs_11_), calls=%async_computation.3 | async-start | bytes 262144 | tf_op jit(solution)/shard_map/all_to_all | solution.py:475
  79.9 0.7 copy-start.6
  79.9 0.8 copy-start.7
